TPU v7x, 32 devices: a whole 2x2x4 slice. The times are simulated.
32 devices in a mesh: blk: 8 (over y, x, core), uly: 4 (over z).
Axes of the slice: x: 2, y: 2, z: 4, core: 2. Of those that a mesh axis runs over, the one named last changes fastest.
Arguments:
- queries: bfloat16 [8192, 4096], P(('blk', 'uly')), may hold values from -6 to 6
- keys: bfloat16 [8192, 4096], P(('blk', 'uly')), may hold values from -6 to 6
- values: bfloat16 [8192, 4096], P(('blk', 'uly')), may hold values from -6 to 6
- doc_start: int32 [8192], P('blk'), may hold values from 0 to 8191, as said below
Outputs:
- attended: bfloat16 [8192, 4096], P(('blk', 'uly'))
Inputs may be any that keep to these rules, and one draw needn't show every extreme that they name: doc_start[0] = 0, and for t > 0 doc_start[t] is either t or doc_start[t - 1].
All inputs are finite; a program needn't handle non-finite values.
Results may differ from a plain program's by a relative error of at most 0.0026.
Values may be sent and summed in bfloat16 or wider, within the bound.
No kernel may reach another device: no remote copies, remote signals or barrier semaphores. Data moves between devices by JAX's collectives and lax.ppermute only.
A program may use at most 128 MiB of HBM per device.

v0:
```python
import math

import jax
import jax.numpy as jnp
from jax import lax
from jax.sharding import PartitionSpec as P

HEAD_DIM = 128


def shifted(block, axis, distance):
    devices = range(lax.axis_size(axis))
    route = [(i - distance, i) for i in devices if i - distance in devices]
    return lax.ppermute(block, axis, route)


def previous_rows(key_stretch, value_stretch, window):
    key_prior, value_prior = shifted((key_stretch, value_stretch), "blk", 1)
    return (key_prior[-window:], value_prior[-window:])


def shards(queries, keys, values, doc_start):
    stretch_len = doc_start.shape[0]
    window = stretch_len // 2
    qblock = min(512, stretch_len)
    query_stretch, key_stretch, value_stretch = (
        lax.all_to_all(queries, "uly", split_axis=1, concat_axis=0, tiled=True),
        lax.all_to_all(keys, "uly", split_axis=1, concat_axis=0, tiled=True),
        lax.all_to_all(values, "uly", split_axis=1, concat_axis=0, tiled=True),
    )
    key_prior, value_prior = previous_rows(key_stretch, value_stretch, window)
    group_width = query_stretch.shape[1]
    group_heads = group_width // HEAD_DIM
    query_all = query_stretch.reshape(stretch_len, group_heads, HEAD_DIM)
    keys_wide = jnp.concatenate([key_prior, key_stretch], axis=0).reshape(
        stretch_len + window, group_heads, HEAD_DIM
    )
    values_wide = jnp.concatenate([value_prior, value_stretch], axis=0).reshape(
        stretch_len + window, group_heads, HEAD_DIM
    )
    anchor = lax.axis_index("blk") * stretch_len
    score_scale = 1.0 / math.sqrt(HEAD_DIM)

    def attend_span(first, query_rows, starts, skipped):
        span_len = qblock + window - skipped
        key_rows = lax.dynamic_slice_in_dim(keys_wide, first + skipped, span_len, 0)
        value_rows = lax.dynamic_slice_in_dim(values_wide, first + skipped, span_len, 0)
        query_pos = anchor + first + jnp.arange(qblock, dtype=jnp.int32)
        key_pos = anchor + first - window + skipped + jnp.arange(span_len, dtype=jnp.int32)
        allowed = (
            (key_pos[None, :] <= query_pos[:, None])
            & (key_pos[None, :] > query_pos[:, None] - window)
            & (key_pos[None, :] >= starts[:, None])
        )
        scores = (
            jnp.einsum("qhd,khd->hqk", query_rows, key_rows, preferred_element_type=jnp.float32)
            * score_scale
        )
        scores = jnp.where(allowed[None], scores, -jnp.inf)
        row_max = jnp.max(scores, axis=-1, keepdims=True)
        probs = jnp.exp(scores - row_max)
        totals = jnp.sum(probs, axis=-1)
        weights = probs.astype(jnp.bfloat16)
        mixed = jnp.einsum("hqk,khd->qhd", weights, value_rows, preferred_element_type=jnp.float32)
        mixed = mixed / jnp.transpose(totals)[:, :, None]
        return mixed.astype(jnp.bfloat16).reshape(qblock, group_width)

    def attend_block(block_index):
        first = block_index * qblock
        query_rows = lax.dynamic_slice_in_dim(query_all, first, qblock, 0)
        starts = lax.dynamic_slice_in_dim(doc_start, first, qblock, 0)
        return attend_span(first, query_rows, starts, 0)

    blocks = lax.map(attend_block, jnp.arange(stretch_len // qblock, dtype=jnp.int32))
    result = blocks.reshape(stretch_len, group_width)
    return lax.all_to_all(result, "uly", split_axis=0, concat_axis=1, tiled=True)


def solution(mesh):
    return jax.shard_map(
        shards,
        mesh=mesh,
        in_specs=(
            P(("blk", "uly"), None),
            P(("blk", "uly"), None),
            P(("blk", "uly"), None),
            P("blk"),
        ),
        out_specs=P(("blk", "uly"), None),
        check_vma=False,
    )
```

profile of v0, /device:TPU:0, one launch (start us, length us, event | category | flops | bytes accessed | tf_op | source)
XLA Modules:
  0.0 291.4 jit_solution(4169752614291744157)
XLA Ops:
  0.0 4.1 %copy.40 = bf16[256,4096]{0,1:T(8,128)(2,1)} copy(bf16[256,4096]{1,0:T(8,128)(2,1)} %param.7) | data formatting | bytes 4194304 | tf_op args[1]
  4.1 6.3 %all-to-all-start.2 = ((bf16[256,4,1024]{0,2,1:T(8,128)(2,1)}), bf16[256,4,1024]{0,2,1:T(8,128)(2,1)S(1)}, u32[]{:S(2)}, u32[]{:S(2)}) async-start(bf16[256,4,1024]{0,2,1:T(8,128)(2,1)} %bitcast.51), calls=%async_computation.2 | async-start | bytes 4194304 | tf_op jit(solution)/shard_map/all_to_all | solution.py:28
  10.4 4.1 %copy.37 = bf16[256,4096]{0,1:T(8,128)(2,1)} copy(bf16[256,4096]{1,0:T(8,128)(2,1)} %param.8) | data formatting | bytes 4194304 | tf_op args[2]
  14.5 44.1 %all-to-all-done.2 = bf16[256,4,1024]{0,2,1:T(8,128)(2,1)S(1)} async-done(((bf16[256,4,1024]{0,2,1:T(8,128)(2,1)}), bf16[256,4,1024]{0,2,1:T(8,128)(2,1)S(1)}, u32[]{:S(2)}, u32[]{:S(2)}) %all-to-all-start.2) | async-done | bytes 2097184 | tf_op jit(solution)/shard_map/all_to_all | solution.py:28
  58.6 1.3 copy-done.1
  59.9 4.5 %all-to-all-start = ((bf16[256,4,1024]{0,2,1:T(8,128)(2,1)}), bf16[256,4,1024]{0,2,1:T(8,128)(2,1)}, u32[]{:S(2)}, u32[]{:S(2)}) async-start(bf16[256,4,1024]{0,2,1:T(8,128)(2,1)} %bitcast.50), calls=%async_computation | async-start | bytes 4194304 | tf_op jit(solution)/shard_map/all_to_all | solution.py:29
  64.4 3.2 %copy.74 = bf16[32,4,8,1024]{3,2,0,1:T(8,128)(2,1)} copy(bf16[32,4,8,1024]{3,2,1,0:T(8,128)(2,1)} %bitcast.58) | data formatting | bytes 4194304 | tf_op jit(solution)/shard_map/all_to_all | solution.py:27
  67.5 44.6 %all-to-all-done = bf16[256,4,1024]{0,2,1:T(8,128)(2,1)} async-done(((bf16[256,4,1024]{0,2,1:T(8,128)(2,1)}), bf16[256,4,1024]{0,2,1:T(8,128)(2,1)}, u32[]{:S(2)}, u32[]{:S(2)}) %all-to-all-start) | async-done | bytes 2097184 | tf_op jit(solution)/shard_map/all_to_all | solution.py:29
  112.1 3.6 %all-to-all-start.1 = ((bf16[256,4,1024]{2,0,1:T(8,128)(2,1)}), bf16[256,4,1024]{2,0,1:T(8,128)(2,1)S(1)}, u32[]{:S(2)}, u32[]{:S(2)}) async-start(bf16[256,4,1024]{2,0,1:T(8,128)(2,1)} %bitcast.34), calls=%async_computation.1 | async-start | bytes 4194304 | tf_op jit(solution)/shard_map/all_to_all | solution.py:27
  115.8 4.0 %copy.41 = bf16[4,256,1024]{2,1,0:T(8,128)(2,1)} copy(bf16[4,256,1024]{1,2,0:T(8,128)(2,1)} %bitcast.49) | data formatting | bytes 4194304 | tf_op jit(solution)/shard_map/all_to_all | solution.py:28
  119.8 2.6 collective-permute-start.1
  122.4 4.0 %copy.38 = bf16[256,4,1024]{2,0,1:T(8,128)(2,1)} copy(bf16[256,4,1024]{0,2,1:T(8,128)(2,1)} %all-to-all-done) | data formatting | bytes 4194304 | tf_op jit(solution)/shard_map/all_to_all | solution.py:29
  126.3 4.2 %collective-permute-start = (bf16[1024,1024]{1,0:T(8,128)(2,1)}, bf16[1024,1024]{1,0:T(8,128)(2,1)}, u32[]{:S(2)}, u32[]{:S(2)}) collective-permute-start(bf16[1024,1024]{1,0:T(8,128)(2,1)} %bitcast.45), channel_id=1, source_target_pairs={{0,4},{4,8},{8,12},{12,16},{16,20},{20,24},{24,28},{1,5},{5,9},{9,... | collective-permute-start | bytes 6291464 | tf_op jit(solution)/shard_map/ppermute | solution.py:14
  130.5 3.7 %copy.58 = bf16[128,8,8,128]{3,2,1,0:T(8,128)(2,1)} copy(bf16[128,8,8,128]{3,1,2,0:T(8,128)(2,1)} %bitcast.46) | data formatting | bytes 4194304
  134.2 2.0 copy.60
  136.2 27.2 %all-to-all-done.1 = bf16[256,4,1024]{2,0,1:T(8,128)(2,1)S(1)} async-done(((bf16[256,4,1024]{2,0,1:T(8,128)(2,1)}), bf16[256,4,1024]{2,0,1:T(8,128)(2,1)S(1)}, u32[]{:S(2)}, u32[]{:S(2)}) %all-to-all-start.1) | async-done | bytes 2097184 | tf_op jit(solution)/shard_map/all_to_all | solution.py:27
  163.4 2.0 copy.59
  165.4 1.3 slice.9
  166.7 0.5 copy.42
  167.2 0.8 copy.44
  168.0 1.4 slice_bitcast_fusion
  169.5 0.3 copy.57
  169.9 0.6 copy-done.3
  170.5 9.2 %pad_maximum_fusion = (bf16[1536,8,128]{2,1,0:T(8,128)(2,1)}, bf16[1536,8,128]{2,1,0:T(8,128)(2,1)}) fusion(bf16[1024,8,128]{2,1,0:T(8,128)(2,1)S(1)} %bitcast.54, bf16[512,8,128]{2,1,0:T(8,128)(2,1)S(1)} %bitcast.56, bf16[1024,8,128]{2,1,0:T(8,128)(2,1)S(1)} %bitcast.55, bf16[512,8,128]{2,1,0:T(8,128)(2,1)S(1)} %copy.44), kind=kLoop, calls=%fused_computation.23 | loop fusion | flops 3145728 | bytes 12582912 | tf_op jit(solution)/shard_map/concatenate | solution.py:38
  179.7 52.1 %while.13 = (s32[]{:T(128)}, bf16[2,512,1024]{2,1,0:T(8,128)(2,1)}, s32[2]{0:T(128)S(1)}, bf16[1536,8,128]{2,1,0:T(8,128)(2,1)}, s32[]{:T(128)}, /*index=5*/s32[...) while((s32[]{:T(128)}, bf16[2,512,1024]{2,1,0:T(8,128)(2,1)}, ...), condition=%wide.region_3.4_spmd, body=%wide.region_0.3_spmd.sunk | while | flops 2197284864 | bytes 90282304 | solution.py:74
  179.7 0.6 dynamic_slice.45
  181.0 0.7 compare_and_fusion.2
  181.7 3.9 %constant_dynamic-slice_fusion.5 = (bf16[1024,8,128]{2,1,0:T(8,128)(2,1)S(1)}, bf16[1024,8,128]{2,1,0:T(8,128)(2,1)}) fusion(bf16[1536,8,128]{2,1,0:T(8,128)(2,1)} %get-tuple-element.281, s32[]{:T(128)S(6)} %select_n.45, bf16[1536,8,128]{2,1,0:T(8,128)(2,1)} %get-tuple-element.277), kind=kLoop, calls=%fused_computation.18.clone.1 | loop fusion | bytes 8388612 | tf_op jit(solution)/shard_map/while/body/eval_jaxpr/dynamic_slice | solution.py:46
  185.5 1.3 constant_dynamic-slice_fusion.6
  186.8 3.5 %fusion.24 = (f32[8,512]{1,0:T(8,128)S(1)}, f32[8,512,1024]{2,1,0:T(8,128)S(1)}) fusion(pred[512,1024]{1,0:T(8,128)(4,1)S(1)} %compare_and_fusion.2, bf16[1024,8,128]{2,1,0:T(8,128)(2,1)S(1)} %get-tuple-element.242, bf16[512,8,128]{2,1,0:T(8,128)(2,1)S(1)} %constant_dynamic-slice_fusion.6), kind=kOutput, calls=%fused_computation.2.clone.1 | convolution fusion | flops 1086320640 | bytes 20463616 | tf_op jit(solution)/shard_map/while/body/eval_jaxpr/qhd,khd->hqk/dot_general | solution.py:56
  190.3 4.4 %fusion.25 = f32[8,512]{1,0:T(8,128)S(1)} fusion(f32[8,512,1024]{2,1,0:T(8,128)S(1)} %get-tuple-element.243, f32[8,512]{1,0:T(8,128)S(1)} %get-tuple-element.244, pred[512,1024]{1,0:T(8,128)(4,1)S(1)} %compare_and_fusion.2), kind=kLoop, calls=%fused_computation.3.clone.1 | loop fusion | flops 16773120 | bytes 17334272 | tf_op jit(solution)/shard_map/while/body/eval_jaxpr/reduce_sum | solution.py:62
  194.7 7.8 %fusion.26 = bf16[512,8,128]{0,2,1:T(8,128)(2,1)} fusion(f32[8,512,1024]{2,1,0:T(8,128)S(1)} %get-tuple-element.243, f32[8,512]{1,0:T(8,128)S(1)} %get-tuple-element.244, pred[512,1024]{1,0:T(8,128)(4,1)S(1)} %compare_and_fusion.2, bf16[1024,8,128]{2,1,0:T(8,128)(2,1)} %get-tuple-element.245, f32[512,8]{0,1:T(8,128)S(1)} %bitcast.60), kind=kOutput, calls=%fused_computation.11.clone.1 | convolution fusion | flops 1091567616 | bytes 20480000 | tf_op jit(solution)/shard_map/while/body/eval_jaxpr/hqk,khd->qhd/dot_general | solution.py:64
  202.4 1.6 copy.82
  204.1 0.3 copy-done.4
  204.5 1.3 copy-done.5
  205.8 0.6 dynamic_slice.45
  207.0 0.7 compare_and_fusion.2
  207.7 3.9 %constant_dynamic-slice_fusion.5 = (bf16[1024,8,128]{2,1,0:T(8,128)(2,1)S(1)}, bf16[1024,8,128]{2,1,0:T(8,128)(2,1)}) fusion(bf16[1536,8,128]{2,1,0:T(8,128)(2,1)} %get-tuple-element.281, s32[]{:T(128)S(6)} %select_n.45, bf16[1536,8,128]{2,1,0:T(8,128)(2,1)} %get-tuple-element.277), kind=kLoop, calls=%fused_computation.18.clone.1 | loop fusion | bytes 8388612 | tf_op jit(solution)/shard_map/while/body/eval_jaxpr/dynamic_slice | solution.py:46
  211.6 1.3 constant_dynamic-slice_fusion.6
  212.9 3.4 %fusion.24 = (f32[8,512]{1,0:T(8,128)S(1)}, f32[8,512,1024]{2,1,0:T(8,128)S(1)}) fusion(pred[512,1024]{1,0:T(8,128)(4,1)S(1)} %compare_and_fusion.2, bf16[1024,8,128]{2,1,0:T(8,128)(2,1)S(1)} %get-tuple-element.242, bf16[512,8,128]{2,1,0:T(8,128)(2,1)S(1)} %constant_dynamic-slice_fusion.6), kind=kOutput, calls=%fused_computation.2.clone.1 | convolution fusion | flops 1086320640 | bytes 20463616 | tf_op jit(solution)/shard_map/while/body/eval_jaxpr/qhd,khd->hqk/dot_general | solution.py:56
  216.3 4.4 %fusion.25 = f32[8,512]{1,0:T(8,128)S(1)} fusion(f32[8,512,1024]{2,1,0:T(8,128)S(1)} %get-tuple-element.243, f32[8,512]{1,0:T(8,128)S(1)} %get-tuple-element.244, pred[512,1024]{1,0:T(8,128)(4,1)S(1)} %compare_and_fusion.2), kind=kLoop, calls=%fused_computation.3.clone.1 | loop fusion | flops 16773120 | bytes 17334272 | tf_op jit(solution)/shard_map/while/body/eval_jaxpr/reduce_sum | solution.py:62
  220.7 7.8 %fusion.26 = bf16[512,8,128]{0,2,1:T(8,128)(2,1)} fusion(f32[8,512,1024]{2,1,0:T(8,128)S(1)} %get-tuple-element.243, f32[8,512]{1,0:T(8,128)S(1)} %get-tuple-element.244, pred[512,1024]{1,0:T(8,128)(4,1)S(1)} %compare_and_fusion.2, bf16[1024,8,128]{2,1,0:T(8,128)(2,1)} %get-tuple-element.245, f32[512,8]{0,1:T(8,128)S(1)} %bitcast.60), kind=kOutput, calls=%fused_computation.11.clone.1 | convolution fusion | flops 1091567616 | bytes 20480000 | tf_op jit(solution)/shard_map/while/body/eval_jaxpr/hqk,khd->qhd/dot_general | solution.py:64
  228.5 1.6 copy.82
  230.1 0.3 copy-done.4
  230.5 1.3 copy-done.5
  231.8 52.9 %all_to_all.73 = bf16[4,256,1024]{2,1,0:T(8,128)(2,1)S(1)} all-to-all(bf16[4,256,1024]{2,1,0:T(8,128)(2,1)} %bitcast.59), channel_id=1, replica_groups=mesh['blk'=8,'uly'=4] {'uly'}, dimensions={0} | all-to-all | bytes 4194304 | tf_op jit(solution)/shard_map/all_to_all | solution.py:76
  284.7 2.6 copy.49
  287.3 4.1 %copy.50 = bf16[256,4096]{1,0:T(8,128)(2,1)} copy(bf16[256,4096]{0,1:T(8,128)(2,1)} %bitcast.53) | data formatting | bytes 4194304 | tf_op jit(solution)/shard_map/all_to_all | solution.py:76
  (24 shorter events, 0.6 us)
Async XLA Ops:
  4.1 54.5 %all-to-all-start.2 = ((bf16[256,4,1024]{0,2,1:T(8,128)(2,1)}), bf16[256,4,1024]{0,2,1:T(8,128)(2,1)S(1)}, u32[]{:S(2)}, u32[]{:S(2)}) async-start(bf16[256,4,1024]{0,2,1:T(8,128)(2,1)} %bitcast.51), calls=%async_computation.2 | async-start | bytes 4194304 | tf_op jit(solution)/shard_map/all_to_all | solution.py:28
  58.6 1.3 copy-start.1
  59.9 52.2 %all-to-all-start = ((bf16[256,4,1024]{0,2,1:T(8,128)(2,1)}), bf16[256,4,1024]{0,2,1:T(8,128)(2,1)}, u32[]{:S(2)}, u32[]{:S(2)}) async-start(bf16[256,4,1024]{0,2,1:T(8,128)(2,1)} %bitcast.50), calls=%async_computation | async-start | bytes 4194304 | tf_op jit(solution)/shard_map/all_to_all | solution.py:29
  112.1 51.3 %all-to-all-start.1 = ((bf16[256,4,1024]{2,0,1:T(8,128)(2,1)}), bf16[256,4,1024]{2,0,1:T(8,128)(2,1)S(1)}, u32[]{:S(2)}, u32[]{:S(2)}) async-start(bf16[256,4,1024]{2,0,1:T(8,128)(2,1)} %bitcast.34), calls=%async_computation.1 | async-start | bytes 4194304 | tf_op jit(solution)/shard_map/all_to_all | solution.py:27
  119.8 45.6 %collective-permute-start.1 = (bf16[1024,1024]{1,0:T(8,128)(2,1)}, bf16[1024,1024]{1,0:T(8,128)(2,1)}, u32[]{:S(2)}, u32[]{:S(2)}) collective-permute-start(bf16[1024,1024]{1,0:T(8,128)(2,1)} %bitcast.47), channel_id=1, source_target_pairs={{0,4},{4,8},{8,12},{12,16},{16,20},{20,24},{24,28},{1,5},{5,9},{9,... | collective-permute-start | bytes 6291464 | tf_op jit(solution)/shard_map/ppermute | solution.py:14
  126.3 41.7 %collective-permute-start = (bf16[1024,1024]{1,0:T(8,128)(2,1)}, bf16[1024,1024]{1,0:T(8,128)(2,1)}, u32[]{:S(2)}, u32[]{:S(2)}) collective-permute-start(bf16[1024,1024]{1,0:T(8,128)(2,1)} %bitcast.45), channel_id=1, source_target_pairs={{0,4},{4,8},{8,12},{12,16},{16,20},{20,24},{24,28},{1,5},{5,9},{9,... | collective-permute-start | bytes 6291464 | tf_op jit(solution)/shard_map/ppermute | solution.py:14
  130.5 3.7 %copy-start = (bf16[4,256,1024]{2,1,0:T(8,128)(2,1)S(1)}, bf16[4,256,1024]{2,1,0:T(8,128)(2,1)}, u32[]{:S(2)}) copy-start(bf16[4,256,1024]{2,1,0:T(8,128)(2,1)} %copy.41) | copy-start | bytes 6291460
  168.0 1.9 copy-start.2
  168.0 2.5 copy-start.3
  170.5 9.2 %copy-start.6 = (s32[1024]{0:T(1024)S(1)}, s32[1024]{0:T(1024)}, u32[]{:S(2)}) copy-start(s32[1024]{0:T(1024)} %param.9) | copy-start | bytes 12292
  202.4 1.9 copy-start.4
  204.5 1.3 copy-start.5
  228.5 1.9 copy-start.4
  230.5 1.3 copy-start.5
where the time goes:
time: 292 us; the launch traced here: 291 us
  waiting for transfers between devices  116 us (40%)
  local copies, waits for them, and re-layouts  58.2 us (20%)
  blocking collectives  52.9 us (18%)
  matrix products  22.5 us (8%)
  starting transfers between devices  21.2 us (7%)
  other arithmetic  19.3 us (7%)
    all_to_all x1, blocking collectives, shards(): lax.all_to_all(result, 'uly', split_axis=0, concat_axis=1, tiled=True)  52.9 us
    all_to_all x1, waiting for transfers between devices, shards(): lax.all_to_all(values, 'uly', split_axis=1, concat_axis=0, tiled=True)  44.6 us
    all_to_all x1, waiting for transfers between devices, shards(): lax.all_to_all(keys, 'uly', split_axis=1, concat_axis=0, tiled=True)  44.1 us
    all_to_all x1, waiting for transfers between devices, shards(): lax.all_to_all(queries, 'uly', split_axis=1, concat_axis=0, tiled=True)  27.2 us
    unnamed x17, local copies, waits for them, and re-layouts  19.6 us
    dot_general x2, matrix products, attend_span(): jnp.einsum('hqk,khd->qhd', weights, value_rows, preferred_element_type=jn...  15.6 us
    concatenate x1, other arithmetic, shards(): jnp.concatenate([value_prior, value_stretch], axis=0)  9.2 us
    reduce_sum x2, other arithmetic, attend_span(): totals = jnp.sum(probs, axis=-1)  8.73 us
  transfers between devices with their start and end apart: 5, of which 3 were waited for; matrix products, arithmetic and copies ran while one was open for 9% of the time, Pallas kernels for 0%

commit v1 on v0

v1 whole, which is shorter than its diff:
```python
import functools
import math

import jax
import jax.numpy as jnp
from jax import lax
from jax.experimental import pallas as pl
from jax.experimental.pallas import tpu as pltpu
from jax.sharding import PartitionSpec as P

HEADS = 32
HEAD_DIM = 128
WINDOW = 512
TILE = 128
ROWS = 32
PIECES = 4
BELOW = -1e30


def split_heads(sources, groups, group_heads, piece, piece_heads):
    tokens = sources[0].shape[0]
    wide = piece_heads * HEAD_DIM

    def kernel(*refs):
        ins, out, sems = refs[: len(sources)], refs[len(sources)], refs[len(sources) + 1]
        copies = []
        for at, src in enumerate(ins):
            for g in range(groups):
                first = (g * group_heads + piece * piece_heads) * HEAD_DIM
                copies.append(
                    pltpu.make_async_copy(
                        src.at[:, pl.ds(first, wide)],
                        out.at[g, :, pl.ds(at * wide, wide)],
                        sems.at[at * groups + g],
                    )
                )
        for copy in copies:
            copy.start()
        for copy in copies:
            copy.wait()

    return pl.pallas_call(
        kernel,
        out_shape=jax.ShapeDtypeStruct((groups, tokens, len(sources) * wide), sources[0].dtype),
        in_specs=[pl.BlockSpec(memory_space=pl.ANY)] * len(sources),
        out_specs=pl.BlockSpec(memory_space=pl.ANY),
        scratch_shapes=[pltpu.SemaphoreType.DMA((len(sources) * groups,))],
        cost_estimate=pl.CostEstimate(
            flops=0, bytes_accessed=4 * groups * tokens * len(sources) * wide, transcendentals=0
        ),
        name="split_heads",
    )(*sources)


def join_heads(pieces, group_heads, piece_heads):
    groups, tokens, wide = pieces[0].shape

    def kernel(*refs):
        ins, out, sems = refs[: len(pieces)], refs[len(pieces)], refs[len(pieces) + 1]
        copies = []
        for at, src in enumerate(ins):
            for g in range(groups):
                first = (g * group_heads + at * piece_heads) * HEAD_DIM
                copies.append(
                    pltpu.make_async_copy(
                        src.at[g], out.at[:, pl.ds(first, wide)], sems.at[at * groups + g]
                    )
                )
        for copy in copies:
            copy.start()
        for copy in copies:
            copy.wait()

    return pl.pallas_call(
        kernel,
        out_shape=jax.ShapeDtypeStruct((tokens, groups * group_heads * HEAD_DIM), pieces[0].dtype),
        in_specs=[pl.BlockSpec(memory_space=pl.ANY)] * len(pieces),
        out_specs=pl.BlockSpec(memory_space=pl.ANY),
        scratch_shapes=[pltpu.SemaphoreType.DMA((len(pieces) * groups,))],
        cost_estimate=pl.CostEstimate(
            flops=0, bytes_accessed=4 * len(pieces) * groups * tokens * wide, transcendentals=0
        ),
        name="join_heads",
    )(*pieces)


def pack(blocks, plan, slots):
    _, rows, wide = blocks.shape
    stretches = plan.shape[1]

    def kernel(plan_ref, in_ref, out_ref):
        for b in range(stretches):
            src, dst, count = plan_ref[0, b], plan_ref[1, b], plan_ref[2, b]

            def move(j, carry, src=src, dst=dst):
                out_ref[dst + j] = in_ref[src + j]
                return carry

            lax.fori_loop(0, count, move, 0)

    return pl.pallas_call(
        kernel,
        out_shape=jax.ShapeDtypeStruct((slots, rows, wide), blocks.dtype),
        in_specs=[pl.BlockSpec(memory_space=pltpu.SMEM), pl.BlockSpec(memory_space=pltpu.VMEM)],
        out_specs=pl.BlockSpec(memory_space=pltpu.VMEM),
        compiler_params=pltpu.CompilerParams(vmem_limit_bytes=32 * 1024 * 1024),
        cost_estimate=pl.CostEstimate(
            flops=0, bytes_accessed=2 * (blocks.size + slots * rows * wide), transcendentals=0
        ),
        name="pack_halo",
    )(plan, blocks)


def attention(plan, lows, query, local, near, far, heads):
    stretches, tokens, wide = query.shape
    tiles = tokens // TILE
    most = WINDOW // TILE + 1
    halo = WINDOW // ROWS
    chunk = tokens // ROWS
    scale = math.log2(math.e) / math.sqrt(HEAD_DIM)

    def kernel(plan_ref, lows_ref, q_ref, local_ref, near_ref, far_ref, out_ref, held):
        b = pl.program_id(0)

        @pl.when(b == 0)
        def _():
            held[...] = jnp.zeros_like(held)

        held[halo:] = local_ref[0].reshape(chunk, ROWS, 2 * wide)
        for ref, at, end in ((near_ref, 0, halo), (far_ref, 2, halo - chunk)):
            first, count = plan_ref[at, b], plan_ref[at + 1, b]

            def move(j, carry, ref=ref, first=first, to=end - count):
                held[to + j] = ref[first + j]
                return carry

            lax.fori_loop(0, count, move, 0)

        for i in range(tiles):
            need = plan_ref[4 + i, b]
            low = jnp.broadcast_to(lows_ref[0, :, i * TILE : (i + 1) * TILE], (TILE, TILE)).T
            for m in range(1, most + 1):

                @pl.when(need == m)
                def _(i=i, m=m, low=low):
                    first = WINDOW + (i + 1 - m) * TILE
                    at = lax.broadcasted_iota(jnp.int32, (TILE, TILE), 1)
                    row = lax.broadcasted_iota(jnp.int32, (TILE, TILE), 0)
                    bias = []
                    for j in range(m):
                        allowed = (at + (first + j * TILE)).astype(jnp.float32) >= low
                        if j == m - 1:
                            allowed = allowed & (at <= row)
                        bias.append(jnp.where(allowed, 0.0, BELOW))
                    bias = jnp.concatenate(bias, axis=1)
                    span = pl.ds(first // ROWS, m * TILE // ROWS)
                    for h in range(heads):
                        q = q_ref[0, i * TILE : (i + 1) * TILE, h * HEAD_DIM : (h + 1) * HEAD_DIM]
                        k = held[span, :, h * HEAD_DIM : (h + 1) * HEAD_DIM].reshape(m * TILE, HEAD_DIM)
                        v = held[span, :, wide + h * HEAD_DIM : wide + (h + 1) * HEAD_DIM].reshape(
                            m * TILE, HEAD_DIM
                        )
                        scores = bias + lax.dot_general(
                            q, k, (((1,), (1,)), ((), ())), preferred_element_type=jnp.float32
                        )
                        row_max = jnp.max(scores, axis=1, keepdims=True)
                        probs = jnp.exp2((scores - row_max) * scale)
                        totals = jnp.sum(probs, axis=1, keepdims=True)
                        mixed = jnp.dot(probs.astype(jnp.bfloat16), v, preferred_element_type=jnp.float32)
                        out_ref[0, i * TILE : (i + 1) * TILE, h * HEAD_DIM : (h + 1) * HEAD_DIM] = (
                            mixed / totals
                        ).astype(jnp.bfloat16)

    whole = lambda array: pl.BlockSpec(array.shape, lambda b: (0,) * array.ndim)
    return pl.pallas_call(
        kernel,
        grid=(stretches,),
        out_shape=jax.ShapeDtypeStruct(query.shape, query.dtype),
        in_specs=[
            pl.BlockSpec(memory_space=pltpu.SMEM),
            pl.BlockSpec((1, 1, tokens), lambda b: (b, 0, 0)),
            pl.BlockSpec((1, tokens, wide), lambda b: (b, 0, 0)),
            pl.BlockSpec((1, tokens, 2 * wide), lambda b: (b, 0, 0)),
            whole(near),
            whole(far),
        ],
        out_specs=pl.BlockSpec((1, tokens, wide), lambda b: (b, 0, 0)),
        scratch_shapes=[pltpu.VMEM((halo + chunk, ROWS, 2 * wide), jnp.bfloat16)],
        compiler_params=pltpu.CompilerParams(
            dimension_semantics=("arbitrary",), vmem_limit_bytes=48 * 1024 * 1024
        ),
        cost_estimate=pl.CostEstimate(
            flops=4 * stretches * tokens * heads * HEAD_DIM * 3 * TILE,
            bytes_accessed=2 * (2 * query.size + local.size + near.size + far.size),
            transcendentals=stretches * tokens * heads * 3 * TILE,
        ),
        name="attention",
    )(plan, lows, query, local, near, far)


def shards(groups, ring, queries, keys, values, doc_start):
    tokens = queries.shape[0]
    group_heads = HEADS // groups
    pieces = min(PIECES, group_heads)
    piece_heads = group_heads // pieces
    chunk = tokens // ROWS
    plane = lax.axis_index("uly")

    starts = lax.all_gather(doc_start, "blk", axis=0, tiled=True)
    chunks = groups * ring
    by_chunk = starts.reshape(chunks, tokens)
    opens = jnp.arange(chunks, dtype=jnp.int32) * tokens
    need = jnp.minimum(opens - by_chunk[:, 0], WINDOW - 1)
    near_need = (jnp.minimum(need, tokens) + ROWS - 1) // ROWS
    far_need = (jnp.maximum(need - tokens, 0) + ROWS - 1) // ROWS
    near_sum = jnp.max(jnp.sum(near_need.reshape(groups, ring), axis=0))
    far_sum = jnp.max(jnp.sum(far_need.reshape(groups, ring), axis=0))

    def mine(per_chunk, ahead):
        padded = jnp.concatenate([per_chunk, jnp.zeros((ring,), jnp.int32)])
        rolled = lax.dynamic_slice_in_dim(padded, plane + ahead, chunks, 0)
        return rolled.reshape(groups, ring)[:, 0]

    def before(counts):
        earlier = jnp.arange(groups)[None, :] < jnp.arange(groups)[:, None]
        return jnp.sum(jnp.where(earlier, counts[None, :], 0), axis=1)

    near_in, far_in = mine(near_need, 0), mine(far_need, 0)
    near_out, far_out = mine(near_need, 1), mine(far_need, 1)
    near_first, far_first = before(near_in), before(far_in)
    own_first = jnp.arange(groups, dtype=jnp.int32) * chunk + chunk - near_out
    near_plan = jnp.stack([own_first, before(near_out), near_out])
    far_plan = jnp.stack([near_first + near_in - far_out, before(far_out), far_out])

    mine_starts = lax.dynamic_index_in_dim(
        starts.reshape(groups, ring, tokens), plane, 1, keepdims=False
    )
    position = (jnp.arange(groups, dtype=jnp.int32)[:, None] * ring + plane) * tokens + jnp.arange(
        tokens, dtype=jnp.int32
    )[None, :]
    window_open = position[:, :1] - WINDOW
    lows = jnp.maximum(mine_starts, position - (WINDOW - 1)) - window_open
    tile_low = lows[:, ::TILE]
    tile_end = WINDOW + TILE * (1 + jnp.arange(tokens // TILE, dtype=jnp.int32))
    tile_need = (tile_end[None, :] - tile_low + TILE - 1) // TILE
    plan = jnp.concatenate(
        [jnp.stack([near_first, near_in, far_first, far_in]), tile_need.T.astype(jnp.int32)]
    )
    lows = lows.astype(jnp.float32)[:, None, :]

    def spread(array):
        return lax.all_to_all(array, "blk", split_axis=0, concat_axis=0, tiled=True)

    def onward(array):
        return lax.ppermute(array, "uly", [(i, (i + 1) % ring) for i in range(ring)])

    def run(near_slots, far_slots, queries, keys, values, near_plan, far_plan, plan, lows):
        done = []
        for piece in range(pieces):
            local = spread(split_heads((keys, values), groups, group_heads, piece, piece_heads))
            blocks = local.reshape(groups * chunk, ROWS, local.shape[2])
            near = onward(pack(blocks, near_plan, near_slots))
            far = onward(pack(near, far_plan, far_slots))
            query = spread(split_heads((queries,), groups, group_heads, piece, piece_heads))
            done.append(spread(attention(plan, lows, query, local, near, far, piece_heads)))
        return join_heads(done, group_heads, piece_heads)

    full = groups * chunk
    return run(full, full, queries, keys, values, near_plan, far_plan, plan, lows)


def solution(mesh):
    return jax.shard_map(
        functools.partial(shards, mesh.shape["blk"], mesh.shape["uly"]),
        mesh=mesh,
        in_specs=(
            P(("blk", "uly"), None),
            P(("blk", "uly"), None),
            P(("blk", "uly"), None),
            P("blk"),
        ),
        out_specs=P(("blk", "uly"), None),
        check_vma=False,
    )
```

time: 292 us -> 462 us (1.58)
  Pallas kernels: 0 us -> 322 us
  waiting for transfers between devices: 116 us -> 51.8 us
  local copies, waits for them, and re-layouts: 58.2 us -> 5.37 us
  starting transfers between devices: 21.2 us -> 56.4 us
  blocking collectives: 52.9 us -> 23.4 us
  matrix products: 22.5 us -> 0 us
  other arithmetic: 19.3 us -> 0.74 us
    pallas_call x0 -> x21, Pallas kernels: none -> 322 us  [the longest x8 200 us: split_heads(): pl.pallas_call(kernel, out_shape=jax.ShapeDtypeStruct((groups, tokens, le...]
    all_to_all x3 -> x11, waiting for transfers between devices: 116 us -> 0.03 us  [spread(): return lax.all_to_all(array, 'blk', split_axis=0, concat_axis=0, tiled=True)]
    ppermute x2 -> x8, waiting for transfers between devices: 0.01 us -> 51.8 us  [onward(): lax.ppermute(array, 'uly', [(i, (i + 1) % ring) for i in range(ring)])]
    all_to_all x1, blocking collectives: 52.9 us -> 13.9 us  [spread(): return lax.all_to_all(array, 'blk', split_axis=0, concat_axis=0, tiled=True)]
    all_to_all x3 -> x11, starting transfers between devices: 14.4 us -> 46.5 us  [spread(): return lax.all_to_all(array, 'blk', split_axis=0, concat_axis=0, tiled=True)]
    dot_general x4 -> x0, matrix products: 22.5 us -> none  [the longest x2 15.6 us: attend_span(): jnp.einsum('hqk,khd->qhd', weights, value_rows, preferred_element_type=jn...]
    all_to_all x5 -> x0, local copies, waits for them, and re-layouts: 17.8 us -> none  [the longest x2 6.66 us: shards(): lax.all_to_all(result, 'uly', split_axis=0, concat_axis=1, tiled=True)]
    unnamed x17 -> x16, local copies, waits for them, and re-layouts: 19.6 us -> 4.21 us
  transfers between devices with their start and end apart: 5 -> 19, of which waited for: 3 -> 5; matrix products, arithmetic and copies ran while one was open for 9% -> 0% of each run, Pallas kernels for 0% -> 52%
where the time goes in v1:
time: 462 us; the launch traced here: 461 us
  Pallas kernels  322 us (70%)
  starting transfers between devices  56.4 us (12%)
  waiting for transfers between devices  51.8 us (11%)
  blocking collectives  23.4 us (5%)
  local copies, waits for them, and re-layouts  5.37 us (1%)
    pallas_call x8, Pallas kernels, split_heads(): pl.pallas_call(kernel, out_shape=jax.ShapeDtypeStruct((groups, tokens, le...  200 us
    pallas_call x1, Pallas kernels, join_heads(): pl.pallas_call(kernel, out_shape=jax.ShapeDtypeStruct((tokens, groups * g...  64.9 us
    ppermute x8, waiting for transfers between devices, onward(): lax.ppermute(array, 'uly', [(i, (i + 1) % ring) for i in range(ring)])  51.8 us
    all_to_all x11, starting transfers between devices, spread(): return lax.all_to_all(array, 'blk', split_axis=0, concat_axis=0, tiled=True)  46.5 us
    pallas_call x4, Pallas kernels, attention(): pl.pallas_call(kernel, grid=(stretches,), out_shape=jax.ShapeDtypeStruct(...  40.3 us
    pallas_call x8, Pallas kernels, pack(): pl.pallas_call(kernel, out_shape=jax.ShapeDtypeStruct((slots, rows, wide)...  16.9 us
    all_to_all x1, blocking collectives, spread(): return lax.all_to_all(array, 'blk', split_axis=0, concat_axis=0, tiled=True)  13.9 us
    ppermute x8, starting transfers between devices, onward(): lax.ppermute(array, 'uly', [(i, (i + 1) % ring) for i in range(ring)])  9.91 us
  transfers between devices with their start and end apart: 19, of which 5 were waited for; matrix products, arithmetic and copies ran while one was open for 0% of the time, Pallas kernels for 52%

profile of v1, /device:TPU:0, one launch (start us, length us, event | category | flops | bytes accessed | tf_op | source)
XLA Modules:
  0.0 460.6 jit_solution(9256217104211323738)
XLA Ops:
  0.0 17.1 %split_heads.14 = bf16[8,256,128]{2,1,0:T(8,128)(2,1)} custom-call(bf16[256,4096]{1,0:T(8,128)(2,1)} %refs_0_.14), custom_call_target="tpu_custom_call" | custom-call | bytes 1048576 | tf_op jit(solution)/shard_map/split_heads/pallas_call | solution.py:42
  17.1 5.2 %all-to-all-start.9 = ((bf16[8,256,128]{2,1,0:T(8,128)(2,1)}), bf16[8,256,128]{2,1,0:T(8,128)(2,1)S(1)}, u32[]{:S(2)}, u32[]{:S(2)}) async-start(bf16[8,256,128]{2,1,0:T(8,128)(2,1)} %split_heads.14), calls=%async_computation.9 | async-start | bytes 1048576 | tf_op jit(solution)/shard_map/all_to_all | solution.py:252
  22.2 17.1 %split_heads.10 = bf16[8,256,128]{2,1,0:T(8,128)(2,1)} custom-call(bf16[256,4096]{1,0:T(8,128)(2,1)} %refs_0_.14), custom_call_target="tpu_custom_call" | custom-call | bytes 1048576 | tf_op jit(solution)/shard_map/split_heads/pallas_call | solution.py:42
  40.1 4.2 all-to-all-start.3
  44.3 33.0 %split_heads.15 = bf16[8,256,256]{2,1,0:T(8,128)(2,1)} custom-call(bf16[256,4096]{1,0:T(8,128)(2,1)} %refs_0_.15, bf16[256,4096]{1,0:T(8,128)(2,1)} %refs_1_.7), custom_call_target="tpu_custom_call" | custom-call | bytes 2097152 | tf_op jit(solution)/shard_map/split_heads/pallas_call | solution.py:42
  77.3 4.2 all-to-all-start.10
  81.6 33.0 %split_heads.11 = bf16[8,256,256]{2,1,0:T(8,128)(2,1)} custom-call(bf16[256,4096]{1,0:T(8,128)(2,1)} %refs_0_.15, bf16[256,4096]{1,0:T(8,128)(2,1)} %refs_1_.7), custom_call_target="tpu_custom_call" | custom-call | bytes 2097152 | tf_op jit(solution)/shard_map/split_heads/pallas_call | solution.py:42
  114.6 4.2 all-to-all-start.4
  118.8 33.0 %split_heads.13 = bf16[8,256,256]{2,1,0:T(8,128)(2,1)} custom-call(bf16[256,4096]{1,0:T(8,128)(2,1)} %refs_0_.15, bf16[256,4096]{1,0:T(8,128)(2,1)} %refs_1_.7), custom_call_target="tpu_custom_call" | custom-call | bytes 2097152 | tf_op jit(solution)/shard_map/split_heads/pallas_call | solution.py:42
  151.8 9.6 %all_gather.3 = s32[8192]{0:T(1024)S(1)} all-gather(s32[1024]{0:T(1024)S(1)} %copy-done.7), channel_id=1, replica_groups=mesh['blk'=8,'uly'=4] {'blk'}, dimensions={0}, use_global_device_ids=true | all-gather | bytes 36864 | tf_op jit(solution)/shard_map/all_gather | solution.py:209
  161.6 3.6 all-to-all-start.7
  165.7 1.7 pack_halo.14
  167.4 1.6 collective-permute-start.6
  169.1 33.0 %split_heads.9 = bf16[8,256,256]{2,1,0:T(8,128)(2,1)} custom-call(bf16[256,4096]{1,0:T(8,128)(2,1)} %refs_0_.15, bf16[256,4096]{1,0:T(8,128)(2,1)} %refs_1_.7), custom_call_target="tpu_custom_call" | custom-call | bytes 2097152 | tf_op jit(solution)/shard_map/split_heads/pallas_call | solution.py:42
  202.4 4.3 all-to-all-start.1
  206.8 1.8 pack_halo.10
  208.6 1.7 collective-permute-start.2
  210.3 1.7 pack_halo.12
  212.0 1.6 collective-permute-start.4
  213.7 2.3 pack_halo.15
  216.2 17.1 %split_heads.12 = bf16[8,256,128]{2,1,0:T(8,128)(2,1)} custom-call(bf16[256,4096]{1,0:T(8,128)(2,1)} %refs_0_.14), custom_call_target="tpu_custom_call" | custom-call | bytes 1048576 | tf_op jit(solution)/shard_map/split_heads/pallas_call | solution.py:42
  233.3 4.2 all-to-all-start.6
  237.7 2.4 pack_halo.8
  240.1 1.5 collective-permute-start
  241.6 2.4 pack_halo.11
  244.0 1.7 collective-permute-start.3
  245.7 17.1 %split_heads.8 = bf16[8,256,128]{2,1,0:T(8,128)(2,1)} custom-call(bf16[256,4096]{1,0:T(8,128)(2,1)} %refs_0_.14), custom_call_target="tpu_custom_call" | custom-call | bytes 1048576 | tf_op jit(solution)/shard_map/split_heads/pallas_call | solution.py:42
  262.9 4.2 all-to-all-start
  267.1 2.3 pack_halo.13
  269.4 1.6 collective-permute-start.5
  271.3 10.3 %collective-permute-done.7.far_ref = bf16[64,32,256]{2,1,0:T(8,128)(2,1)} collective-permute-done((bf16[64,32,256]{2,1,0:T(8,128)(2,1)}, bf16[64,32,256]{2,1,0:T(8,128)(2,1)}, u32[]{:S(2)}, u32[]{:S(2)}) %collective-permute-start.7) | collective-permute-done | bytes 1048608 | tf_op jit(solution)/shard_map/ppermute | solution.py:255
  281.6 1.0 copy-done.3
  282.7 9.8 %attention.7 = bf16[8,256,128]{2,1,0:T(8,128)(2,1)S(1)} custom-call(s32[6,8]{1,0:T(8,128)S(1)} %concatenate.13.plan_ref, f32[8,1,256]{2,1,0:T(1,128)S(1)} %get-tuple-element.5.lows_ref, bf16[8,256,128]{2,1,0:T(8,128)(2,1)S(1)} %copy-done.3, bf16[8,256,256]{2,1,0:T(8,128)(2,1)S(1)} %all-to-all-done.10.local_ref, ...), custom_call_target="tpu_custom_call" | custom-call | flops 402653184 | bytes 4194304 | tf_op jit(solution)/shard_map/attention/pallas_call | solution.py:175
  292.5 0.8 copy-done.4
  293.3 4.3 all-to-all-start.11
  297.6 6.5 %collective-permute-done.in_ref.near_ref = bf16[64,32,256]{2,1,0:T(8,128)(2,1)} collective-permute-done((bf16[64,32,256]{2,1,0:T(8,128)(2,1)}, bf16[64,32,256]{2,1,0:T(8,128)(2,1)}, u32[]{:S(2)}, u32[]{:S(2)}) %collective-permute-start) | collective-permute-done | bytes 1048608 | tf_op jit(solution)/shard_map/ppermute | solution.py:255
  304.1 2.3 pack_halo.9
  306.4 20.2 %collective-permute-done.3.far_ref = bf16[64,32,256]{2,1,0:T(8,128)(2,1)} collective-permute-done((bf16[64,32,256]{2,1,0:T(8,128)(2,1)}, bf16[64,32,256]{2,1,0:T(8,128)(2,1)}, u32[]{:S(2)}, u32[]{:S(2)}) %collective-permute-start.3) | collective-permute-done | bytes 1048608 | tf_op jit(solution)/shard_map/ppermute | solution.py:255
  326.6 10.5 %attention.5 = bf16[8,256,128]{2,1,0:T(8,128)(2,1)} custom-call(s32[6,8]{1,0:T(8,128)S(1)} %concatenate.13.plan_ref, f32[8,1,256]{2,1,0:T(1,128)S(1)} %get-tuple-element.5.lows_ref, bf16[8,256,128]{2,1,0:T(8,128)(2,1)S(1)} %copy-done.1, bf16[8,256,256]{2,1,0:T(8,128)(2,1)S(1)} %all-to-all-done.4.local_ref, ...), custom_call_target="tpu_custom_call" | custom-call | flops 402653184 | bytes 4194304 | tf_op jit(solution)/shard_map/attention/pallas_call | solution.py:175
  337.1 4.1 all-to-all-start.5
  341.2 7.8 %collective-permute-done.5.far_ref = bf16[64,32,256]{2,1,0:T(8,128)(2,1)} collective-permute-done((bf16[64,32,256]{2,1,0:T(8,128)(2,1)}, bf16[64,32,256]{2,1,0:T(8,128)(2,1)}, u32[]{:S(2)}, u32[]{:S(2)}) %collective-permute-start.5) | collective-permute-done | bytes 1048608 | tf_op jit(solution)/shard_map/ppermute | solution.py:255
  349.0 10.0 %attention.6 = bf16[8,256,128]{2,1,0:T(8,128)(2,1)S(1)} custom-call(s32[6,8]{1,0:T(8,128)S(1)} %concatenate.13.plan_ref, f32[8,1,256]{2,1,0:T(1,128)S(1)} %get-tuple-element.5.lows_ref, bf16[8,256,128]{2,1,0:T(8,128)(2,1)} %all-to-all-done.6.q_ref, bf16[8,256,256]{2,1,0:T(8,128)(2,1)S(1)} %all-to-all-done.7.local_ref, ...), custom_call_target="tpu_custom_call" | custom-call | flops 402653184 | bytes 4194304 | tf_op jit(solution)/shard_map/attention/pallas_call | solution.py:175
  359.0 0.8 copy-done.5
  359.8 4.1 all-to-all-start.8
  363.9 7.0 %collective-permute-done.1.far_ref = bf16[64,32,256]{2,1,0:T(8,128)(2,1)} collective-permute-done((bf16[64,32,256]{2,1,0:T(8,128)(2,1)}, bf16[64,32,256]{2,1,0:T(8,128)(2,1)}, u32[]{:S(2)}, u32[]{:S(2)}) %collective-permute-start.1) | collective-permute-done | bytes 1048608 | tf_op jit(solution)/shard_map/ppermute | solution.py:255
  370.9 10.0 %attention.4 = bf16[8,256,128]{2,1,0:T(8,128)(2,1)S(1)} custom-call(s32[6,8]{1,0:T(8,128)S(1)} %concatenate.13.plan_ref, f32[8,1,256]{2,1,0:T(1,128)S(1)} %get-tuple-element.5.lows_ref, bf16[8,256,128]{2,1,0:T(8,128)(2,1)} %all-to-all-done.q_ref, bf16[8,256,256]{2,1,0:T(8,128)(2,1)} %all-to-all-done.1.local_ref, ...), custom_call_target="tpu_custom_call" | custom-call | flops 402653184 | bytes 4194304 | tf_op jit(solution)/shard_map/attention/pallas_call | solution.py:175
  381.8 13.9 %all_to_all.60.refs_0_ = bf16[8,256,128]{2,1,0:T(8,128)(2,1)} all-to-all(bf16[8,256,128]{2,1,0:T(8,128)(2,1)} %copy-done.6), channel_id=1, replica_groups=mesh['blk'=8,'uly'=4] {'blk'}, dimensions={0} | all-to-all | bytes 1048576 | tf_op jit(solution)/shard_map/all_to_all | solution.py:252
  395.6 64.9 %join_heads.1 = bf16[256,4096]{1,0:T(8,128)(2,1)} custom-call(bf16[8,256,128]{2,1,0:T(8,128)(2,1)} %all_to_all.60.refs_0_, bf16[8,256,128]{2,1,0:T(8,128)(2,1)} %all-to-all-done.5.refs_1_, bf16[8,256,128]{2,1,0:T(8,128)(2,1)} %all-to-all-done.8.refs_2_, bf16[8,256,128]{2,1,0:T(8,128)(2,1)} %all-to-all-done.11.refs_3_), custom_call_target="tpu_custom_call" | custom-call | bytes 4194304 | tf_op jit(solution)/shard_map/join_heads/pallas_call | solution.py:74
  (60 shorter events, 3.8 us)
Async XLA Ops:
  17.1 22.2 %all-to-all-start.9 = ((bf16[8,256,128]{2,1,0:T(8,128)(2,1)}), bf16[8,256,128]{2,1,0:T(8,128)(2,1)S(1)}, u32[]{:S(2)}, u32[]{:S(2)}) async-start(bf16[8,256,128]{2,1,0:T(8,128)(2,1)} %split_heads.14), calls=%async_computation.9 | async-start | bytes 1048576 | tf_op jit(solution)/shard_map/all_to_all | solution.py:252
  39.3 0.8 copy-start.2
  40.1 37.2 %all-to-all-start.3 = ((bf16[8,256,128]{2,1,0:T(8,128)(2,1)}), bf16[8,256,128]{2,1,0:T(8,128)(2,1)S(1)}, u32[]{:S(2)}, u32[]{:S(2)}) async-start(bf16[8,256,128]{2,1,0:T(8,128)(2,1)} %split_heads.10), calls=%async_computation.3 | async-start | bytes 1048576 | tf_op jit(solution)/shard_map/all_to_all | solution.py:252
  77.3 37.2 %copy-start = (bf16[8,256,128]{2,1,0:T(8,128)(2,1)}, bf16[8,256,128]{2,1,0:T(8,128)(2,1)S(1)}, u32[]{:S(2)}) copy-start(bf16[8,256,128]{2,1,0:T(8,128)(2,1)S(1)} %all-to-all-done.3.q_ref) | copy-start | bytes 1572868
  77.3 37.2 %all-to-all-start.10 = ((bf16[8,256,256]{2,1,0:T(8,128)(2,1)}), bf16[8,256,256]{2,1,0:T(8,128)(2,1)S(1)}, u32[]{:S(2)}, u32[]{:S(2)}) async-start(bf16[8,256,256]{2,1,0:T(8,128)(2,1)} %split_heads.15), calls=%async_computation.10 | async-start | bytes 2097152 | tf_op jit(solution)/shard_map/all_to_all | solution.py:252
  114.6 47.0 %all-to-all-start.4 = ((bf16[8,256,256]{2,1,0:T(8,128)(2,1)}), bf16[8,256,256]{2,1,0:T(8,128)(2,1)S(1)}, u32[]{:S(2)}, u32[]{:S(2)}) async-start(bf16[8,256,256]{2,1,0:T(8,128)(2,1)} %split_heads.11), calls=%async_computation.4 | async-start | bytes 2097152 | tf_op jit(solution)/shard_map/all_to_all | solution.py:252
  118.8 33.0 %copy-start.7 = (s32[1024]{0:T(1024)S(1)}, s32[1024]{0:T(1024)}, u32[]{:S(2)}) copy-start(s32[1024]{0:T(1024)} %param.7) | copy-start | bytes 12292
  161.6 40.8 %all-to-all-start.7 = ((bf16[8,256,256]{2,1,0:T(8,128)(2,1)}), bf16[8,256,256]{2,1,0:T(8,128)(2,1)S(1)}, u32[]{:S(2)}, u32[]{:S(2)}) async-start(bf16[8,256,256]{2,1,0:T(8,128)(2,1)} %split_heads.13), calls=%async_computation.7 | async-start | bytes 2097152 | tf_op jit(solution)/shard_map/all_to_all | solution.py:252
  167.4 46.3 %collective-permute-start.6 = (bf16[64,32,256]{2,1,0:T(8,128)(2,1)}, bf16[64,32,256]{2,1,0:T(8,128)(2,1)}, u32[]{:S(2)}, u32[]{:S(2)}) collective-permute-start(bf16[64,32,256]{2,1,0:T(8,128)(2,1)} %pack_halo.14), channel_id=1, source_target_pairs={{0,1},{1,2},{2,3},{3,0},{4,5},{5,6},{6,7},{7,4},{8,9},{9,10},{10,1... | collective-permute-start | bytes 3145736 | tf_op jit(solution)/shard_map/ppermute | solution.py:255
  202.4 30.8 %all-to-all-start.1 = ((bf16[8,256,256]{2,1,0:T(8,128)(2,1)}), bf16[8,256,256]{2,1,0:T(8,128)(2,1)}, u32[]{:S(2)}, u32[]{:S(2)}) async-start(bf16[8,256,256]{2,1,0:T(8,128)(2,1)} %split_heads.9), calls=%async_computation.1 | async-start | bytes 2097152 | tf_op jit(solution)/shard_map/all_to_all | solution.py:252
  208.6 33.0 %collective-permute-start.2 = (bf16[64,32,256]{2,1,0:T(8,128)(2,1)}, bf16[64,32,256]{2,1,0:T(8,128)(2,1)}, u32[]{:S(2)}, u32[]{:S(2)}) collective-permute-start(bf16[64,32,256]{2,1,0:T(8,128)(2,1)} %pack_halo.10), channel_id=1, source_target_pairs={{0,1},{1,2},{2,3},{3,0},{4,5},{5,6},{6,7},{7,4},{8,9},{9,10},{10,1... | collective-permute-start | bytes 3145736 | tf_op jit(solution)/shard_map/ppermute | solution.py:255
  212.0 55.1 %collective-permute-start.4 = (bf16[64,32,256]{2,1,0:T(8,128)(2,1)}, bf16[64,32,256]{2,1,0:T(8,128)(2,1)}, u32[]{:S(2)}, u32[]{:S(2)}) collective-permute-start(bf16[64,32,256]{2,1,0:T(8,128)(2,1)} %pack_halo.12), channel_id=1, source_target_pairs={{0,1},{1,2},{2,3},{3,0},{4,5},{5,6},{6,7},{7,4},{8,9},{9,10},{10,1... | collective-permute-start | bytes 3145736 | tf_op jit(solution)/shard_map/ppermute | solution.py:255
  216.0 65.6 %collective-permute-start.7 = (bf16[64,32,256]{2,1,0:T(8,128)(2,1)}, bf16[64,32,256]{2,1,0:T(8,128)(2,1)}, u32[]{:S(2)}, u32[]{:S(2)}) collective-permute-start(bf16[64,32,256]{2,1,0:T(8,128)(2,1)} %pack_halo.15), channel_id=1, source_target_pairs={{0,1},{1,2},{2,3},{3,0},{4,5},{5,6},{6,7},{7,4},{8,9},{9,10},{10,1... | collective-permute-start | bytes 3145736 | tf_op jit(solution)/shard_map/ppermute | solution.py:255
  233.3 29.6 %all-to-all-start.6 = ((bf16[8,256,128]{2,1,0:T(8,128)(2,1)}), bf16[8,256,128]{2,1,0:T(8,128)(2,1)}, u32[]{:S(2)}, u32[]{:S(2)}) async-start(bf16[8,256,128]{2,1,0:T(8,128)(2,1)} %split_heads.12), calls=%async_computation.6 | async-start | bytes 1048576 | tf_op jit(solution)/shard_map/all_to_all | solution.py:252
  240.1 64.0 %collective-permute-start = (bf16[64,32,256]{2,1,0:T(8,128)(2,1)}, bf16[64,32,256]{2,1,0:T(8,128)(2,1)}, u32[]{:S(2)}, u32[]{:S(2)}) collective-permute-start(bf16[64,32,256]{2,1,0:T(8,128)(2,1)} %pack_halo.8), channel_id=1, source_target_pairs={{0,1},{1,2},{2,3},{3,0},{4,5},{5,6},{6,7},{7,4},{8,9},{9,10},{10,1... | collective-permute-start | bytes 3145736 | tf_op jit(solution)/shard_map/ppermute | solution.py:255
  244.0 82.6 %collective-permute-start.3 = (bf16[64,32,256]{2,1,0:T(8,128)(2,1)}, bf16[64,32,256]{2,1,0:T(8,128)(2,1)}, u32[]{:S(2)}, u32[]{:S(2)}) collective-permute-start(bf16[64,32,256]{2,1,0:T(8,128)(2,1)} %pack_halo.11), channel_id=1, source_target_pairs={{0,1},{1,2},{2,3},{3,0},{4,5},{5,6},{6,7},{7,4},{8,9},{9,10},{10,1... | collective-permute-start | bytes 3145736 | tf_op jit(solution)/shard_map/ppermute | solution.py:255
  262.9 30.4 %all-to-all-start = ((bf16[8,256,128]{2,1,0:T(8,128)(2,1)}), bf16[8,256,128]{2,1,0:T(8,128)(2,1)}, u32[]{:S(2)}, u32[]{:S(2)}) async-start(bf16[8,256,128]{2,1,0:T(8,128)(2,1)} %split_heads.8), calls=%async_computation | async-start | bytes 1048576 | tf_op jit(solution)/shard_map/all_to_all | solution.py:252
  269.4 79.6 %collective-permute-start.5 = (bf16[64,32,256]{2,1,0:T(8,128)(2,1)}, bf16[64,32,256]{2,1,0:T(8,128)(2,1)}, u32[]{:S(2)}, u32[]{:S(2)}) collective-permute-start(bf16[64,32,256]{2,1,0:T(8,128)(2,1)} %pack_halo.13), channel_id=1, source_target_pairs={{0,1},{1,2},{2,3},{3,0},{4,5},{5,6},{6,7},{7,4},{8,9},{9,10},{10,1... | collective-permute-start | bytes 3145736 | tf_op jit(solution)/shard_map/ppermute | solution.py:255
  281.6 1.0 copy-start.3
  292.5 0.8 copy-start.4
  293.3 33.3 %copy-start.1 = (bf16[8,256,128]{2,1,0:T(8,128)(2,1)S(1)}, bf16[8,256,128]{2,1,0:T(8,128)(2,1)}, u32[]{:S(2)}) copy-start(bf16[8,256,128]{2,1,0:T(8,128)(2,1)} %copy-done) | copy-start | bytes 1572868
  293.3 43.8 %all-to-all-start.11 = ((bf16[8,256,128]{2,1,0:T(8,128)(2,1)}), bf16[8,256,128]{2,1,0:T(8,128)(2,1)}, u32[]{:S(2)}, u32[]{:S(2)}) async-start(bf16[8,256,128]{2,1,0:T(8,128)(2,1)} %copy-done.4), calls=%async_computation.11 | async-start | bytes 1048576 | tf_op jit(solution)/shard_map/all_to_all | solution.py:252
  306.4 64.6 %collective-permute-start.1 = (bf16[64,32,256]{2,1,0:T(8,128)(2,1)}, bf16[64,32,256]{2,1,0:T(8,128)(2,1)}, u32[]{:S(2)}, u32[]{:S(2)}) collective-permute-start(bf16[64,32,256]{2,1,0:T(8,128)(2,1)} %pack_halo.9), channel_id=1, source_target_pairs={{0,1},{1,2},{2,3},{3,0},{4,5},{5,6},{6,7},{7,4},{8,9},{9,10},{10,1... | collective-permute-start | bytes 3145736 | tf_op jit(solution)/shard_map/ppermute | solution.py:255
  337.1 22.7 %all-to-all-start.5 = ((bf16[8,256,128]{2,1,0:T(8,128)(2,1)}), bf16[8,256,128]{2,1,0:T(8,128)(2,1)}, u32[]{:S(2)}, u32[]{:S(2)}) async-start(bf16[8,256,128]{2,1,0:T(8,128)(2,1)} %attention.5), calls=%async_computation.5 | async-start | bytes 1048576 | tf_op jit(solution)/shard_map/all_to_all | solution.py:252
  359.0 0.8 copy-start.5
  359.8 22.0 %all-to-all-start.8 = ((bf16[8,256,128]{2,1,0:T(8,128)(2,1)}), bf16[8,256,128]{2,1,0:T(8,128)(2,1)}, u32[]{:S(2)}, u32[]{:S(2)}) async-start(bf16[8,256,128]{2,1,0:T(8,128)(2,1)} %copy-done.5), calls=%async_computation.8 | async-start | bytes 1048576 | tf_op jit(solution)/shard_map/all_to_all | solution.py:252
  381.0 0.8 copy-start.6

commit v2 on v0

v2 whole, which is shorter than its diff:
```python
import functools
import math

import jax
import jax.numpy as jnp
from jax import lax
from jax.experimental import pallas as pl
from jax.experimental.pallas import tpu as pltpu
from jax.sharding import PartitionSpec as P

HEADS = 32
HEAD_DIM = 128
WINDOW = 512
TILE = 128
ROWS = 32
BELOW = -1e30
UNROLLED = 3
SIZES = {3: (1, 2)}
ROOMS = ((34, 10), (38, 17), (46, 19), (51, 28), (64, 64))


def split_heads(sources, groups, group_heads):
    tokens, columns = sources[0].shape
    wide = group_heads * HEAD_DIM
    rest = columns - groups * wide
    rows = min(2 * ROWS, tokens)

    def kernel(*refs):
        ins, out, other = refs[: len(sources)], refs[-2], refs[-1]
        for at, src in enumerate(ins):
            for g in range(groups):
                out[g, :, at * wide : (at + 1) * wide] = src[:, g * wide : (g + 1) * wide]
            other[0, :, at * rest : (at + 1) * rest] = src[:, groups * wide :]

    widths = (len(sources) * wide, len(sources) * rest)
    return pl.pallas_call(
        kernel,
        grid=(tokens // rows,),
        out_shape=[
            jax.ShapeDtypeStruct((groups, tokens, widths[0]), sources[0].dtype),
            jax.ShapeDtypeStruct((1, tokens, widths[1]), sources[0].dtype),
        ],
        in_specs=[pl.BlockSpec((rows, columns), lambda t: (t, 0))] * len(sources),
        out_specs=[
            pl.BlockSpec((groups, rows, widths[0]), lambda t: (0, t, 0)),
            pl.BlockSpec((1, rows, widths[1]), lambda t: (0, t, 0)),
        ],
        cost_estimate=pl.CostEstimate(
            flops=0, bytes_accessed=4 * len(sources) * sources[0].size, transcendentals=0
        ),
        name="split_heads",
    )(*sources)


def join_heads(pieces, rest):
    groups, tokens, _ = pieces[0].shape
    band = sum(piece.shape[2] for piece in pieces)
    rows = min(2 * ROWS, tokens)

    def kernel(*refs):
        ins, other, out = refs[:-2], refs[-2], refs[-1]
        for g in range(groups):
            first = g * band
            for src in ins:
                out[:, first : first + src.shape[2]] = src[g]
                first += src.shape[2]
        out[:, groups * band :] = other[0]

    columns = groups * band + rest.shape[2]
    return pl.pallas_call(
        kernel,
        grid=(tokens // rows,),
        out_shape=jax.ShapeDtypeStruct((tokens, columns), rest.dtype),
        in_specs=[
            pl.BlockSpec((piece.shape[0], rows, piece.shape[2]), lambda t: (0, t, 0))
            for piece in (*pieces, rest)
        ],
        out_specs=pl.BlockSpec((rows, columns), lambda t: (t, 0)),
        cost_estimate=pl.CostEstimate(flops=0, bytes_accessed=4 * tokens * columns, transcendentals=0),
        name="join_heads",
    )(*pieces, rest)


def pack(blocks, plan, slots, bands):
    _, rows, _ = blocks.shape
    stretches = plan.shape[1]
    wide = sum(end - first for first, end in bands)

    def kernel(plan_ref, in_ref, out_ref):
        def stretch(b, carry):
            src, dst, count = plan_ref[0, b], plan_ref[1, b], plan_ref[2, b]

            def move(j, carry):
                to = 0
                for first, end in bands:
                    out_ref[dst + j, :, to : to + end - first] = in_ref[src + j, :, first:end]
                    to += end - first
                return carry

            return lax.fori_loop(0, count, move, carry)

        lax.fori_loop(0, stretches, stretch, 0)

    return pl.pallas_call(
        kernel,
        out_shape=jax.ShapeDtypeStruct((slots, rows, wide), blocks.dtype),
        in_specs=[pl.BlockSpec(memory_space=pltpu.SMEM), pl.BlockSpec(memory_space=pltpu.VMEM)],
        out_specs=pl.BlockSpec(memory_space=pltpu.VMEM),
        compiler_params=pltpu.CompilerParams(vmem_limit_bytes=32 * 1024 * 1024),
        cost_estimate=pl.CostEstimate(
            flops=0, bytes_accessed=4 * slots * rows * wide, transcendentals=0
        ),
        name="pack_halo",
    )(plan, blocks)


def attention(plan, lows, query, query_heads, local, local_bands, near, far):
    start, heads = query_heads
    stretches, tokens, _ = query.shape
    wide = heads * HEAD_DIM
    tiles = tokens // TILE
    most = WINDOW // TILE + 1
    halo = WINDOW // ROWS
    chunk = tokens // ROWS
    scale = math.log2(math.e) / math.sqrt(HEAD_DIM)

    def attend(m, b, lows_ref, q_ref, out_ref, held):
        at = lax.broadcasted_iota(jnp.int32, (TILE, TILE), 1)
        row = lax.broadcasted_iota(jnp.int32, (TILE, TILE), 0)
        spans, biases = [], []
        for i in range(tiles):
            first = WINDOW + (i + 1 - m) * TILE
            low = lows_ref[b, i * TILE : (i + 1) * TILE]
            bias = []
            for j in range(m):
                allowed = (at + (first + j * TILE)).astype(jnp.float32) >= low
                if j == m - 1:
                    allowed = allowed & (at <= row)
                bias.append(jnp.where(allowed, 0.0, BELOW))
            biases.append(jnp.concatenate(bias, axis=1))
            spans.append(pl.ds(first // ROWS, m * TILE // ROWS))

        def head(h, carry):
            at = lambda base: pl.ds(pl.multiple_of((base + h) * HEAD_DIM, HEAD_DIM), HEAD_DIM)
            for i in range(tiles):
                q = q_ref[b, i * TILE : (i + 1) * TILE, at(start)]
                k = held[spans[i], :, at(0)].reshape(m * TILE, HEAD_DIM)
                v = held[spans[i], :, at(heads)].reshape(m * TILE, HEAD_DIM)
                scores = biases[i] + lax.dot_general(
                    q, k, (((1,), (1,)), ((), ())), preferred_element_type=jnp.float32
                )
                row_max = jnp.max(scores, axis=1, keepdims=True)
                probs = jnp.exp2((scores - row_max) * scale)
                totals = jnp.sum(probs, axis=1, keepdims=True)
                mixed = jnp.dot(probs.astype(jnp.bfloat16), v, preferred_element_type=jnp.float32)
                out_ref[b, i * TILE : (i + 1) * TILE, at(0)] = (mixed / totals).astype(jnp.bfloat16)
            return carry

        if heads <= UNROLLED:
            for h in range(heads):
                head(h, 0)
        else:
            lax.fori_loop(0, heads, head, 0)

    def kernel(plan_ref, lows_ref, q_ref, local_ref, near_ref, far_ref, out_ref, held):
        held[...] = jnp.zeros_like(held)

        def stretch(b, carry):
            for at, (first, end) in enumerate(local_bands):
                held[halo:, :, at * wide : (at + 1) * wide] = local_ref[b, :, first:end].reshape(
                    chunk, ROWS, wide
                )
            for ref, at, end in ((near_ref, 0, halo), (far_ref, 2, halo - chunk)):
                first, count = plan_ref[at, b], plan_ref[at + 1, b]

                def move(j, carry, ref=ref, first=first, to=end - count):
                    held[to + j] = ref[first + j]
                    return carry

                lax.fori_loop(0, count, move, 0)

            need = plan_ref[4, b]
            for m in range(1, most + 1):
                pl.when(need == m)(functools.partial(attend, m, b, lows_ref, q_ref, out_ref, held))
            return carry

        lax.fori_loop(0, stretches, stretch, 0)

    return pl.pallas_call(
        kernel,
        out_shape=jax.ShapeDtypeStruct((stretches, tokens, wide), query.dtype),
        in_specs=[pl.BlockSpec(memory_space=pltpu.SMEM)] + [pl.BlockSpec(memory_space=pltpu.VMEM)] * 5,
        out_specs=pl.BlockSpec(memory_space=pltpu.VMEM),
        scratch_shapes=[pltpu.VMEM((halo + chunk, ROWS, 2 * wide), jnp.bfloat16)],
        compiler_params=pltpu.CompilerParams(vmem_limit_bytes=32 * 1024 * 1024),
        cost_estimate=pl.CostEstimate(
            flops=4 * stretches * tokens * heads * HEAD_DIM * 3 * TILE,
            bytes_accessed=2 * (4 * stretches * tokens * wide + near.size + far.size),
            transcendentals=stretches * tokens * heads * 3 * TILE,
        ),
        name="attention",
    )(plan, lows, query, local, near, far)


def shards(groups, ring, queries, keys, values, doc_start):
    tokens = queries.shape[0]
    group_heads = max(1, 3 * HEADS // (4 * groups))
    rest_heads = HEADS - groups * group_heads
    chunk = tokens // ROWS
    chunks = groups * ring
    plane = lax.axis_index("uly")
    me = lax.axis_index("blk") * ring + plane

    def spread(array):
        return lax.all_to_all(array, "blk", split_axis=0, concat_axis=0, tiled=True)

    def onward(array):
        return lax.ppermute(array, "uly", [(i, (i + 1) % ring) for i in range(ring)])

    def next_chunk(array):
        return lax.ppermute(array, ("blk", "uly"), [(i, i + 1) for i in range(chunks - 1)])

    starts = spread(jnp.broadcast_to(doc_start[None, None], (groups, 1, ring * tokens)))
    by_chunk = starts.reshape(chunks, tokens)
    opens = jnp.arange(chunks, dtype=jnp.int32) * tokens
    need = jnp.minimum(opens - by_chunk[:, 0], WINDOW - 1)
    near_need = (jnp.minimum(need, tokens) + ROWS - 1) // ROWS
    far_need = (jnp.maximum(need - tokens, 0) + ROWS - 1) // ROWS
    near_sum = jnp.max(jnp.sum(near_need.reshape(groups, ring), axis=0))
    far_sum = jnp.max(jnp.sum(far_need.reshape(groups, ring), axis=0))

    def mine(per_chunk, ahead):
        padded = jnp.concatenate([per_chunk, jnp.zeros((ring,), jnp.int32)])
        rolled = lax.dynamic_slice_in_dim(padded, plane + ahead, chunks, 0)
        return rolled.reshape(groups, ring)[:, 0]

    def before(counts):
        earlier = jnp.arange(groups)[None, :] < jnp.arange(groups)[:, None]
        return jnp.sum(jnp.where(earlier, counts[None, :], 0), axis=1)

    near_in, far_in = mine(near_need, 0), mine(far_need, 0)
    near_out, far_out = mine(near_need, 1), mine(far_need, 1)
    near_first = before(near_in)
    own_first = jnp.arange(groups, dtype=jnp.int32) * chunk + chunk - near_out
    near_plan = jnp.stack([own_first, before(near_out), near_out])
    far_plan = jnp.stack([near_first + near_in - far_out, before(far_out), far_out])

    position = jnp.arange(chunks * tokens, dtype=jnp.int32).reshape(chunks, tokens)
    lows = jnp.maximum(by_chunk, position - (WINDOW - 1)) - (opens[:, None] - WINDOW)
    tile_end = WINDOW + TILE * (1 + jnp.arange(tokens // TILE, dtype=jnp.int32))
    tile_need = jnp.max((tile_end[None, :] - lows[:, ::TILE] + TILE - 1) // TILE, axis=1)
    lows = lows.astype(jnp.float32)
    plane_lows = lax.dynamic_index_in_dim(lows.reshape(groups, ring, tokens), plane, 1, keepdims=False)
    plane_lows = jnp.broadcast_to(plane_lows[:, :, None], (groups, tokens, TILE))
    plan = jnp.stack([near_first, near_in, before(far_in), far_in, mine(tile_need, 0)])

    def own(per_chunk):
        return lax.dynamic_index_in_dim(per_chunk, me, 0, keepdims=False)

    own_near, own_far = own(near_need), own(far_need)
    own_plan = jnp.stack([chunk - own_near, own_near, chunk - own_far, own_far, own(tile_need)])[:, None]
    own_lows = jnp.broadcast_to(own(lows)[None, :, None], (1, tokens, TILE))

    wide, rest = group_heads * HEAD_DIM, rest_heads * HEAD_DIM
    pair, own_pair = split_heads((keys, values), groups, group_heads)
    own_next = next_chunk(own_pair)
    own_after = next_chunk(own_next)
    pair = spread(pair)
    later, _ = lax.optimization_barrier((queries, starts))
    query, own_query = split_heads((later,), groups, group_heads)

    def run(room, pair, query, near_plan, far_plan, plan, plane_lows, own_query, own_pair, own_next, own_after, own_plan, own_lows):
        near_slots, far_slots = (groups * chunk * share // 64 for share in room)
        blocks = pair.reshape(groups * chunk, ROWS, 2 * wide)
        pieces = []
        start = 0
        for size in SIZES.get(group_heads, (group_heads,)):
            first, end = start * HEAD_DIM, (start + size) * HEAD_DIM
            pieces.append(((start, size), ((first, end), (wide + first, wide + end))))
            start += size
        packed = [pack(blocks, near_plan, near_slots, bands) for _, bands in pieces]
        query = spread(lax.optimization_barrier((query, packed))[0])
        nears = [onward(packed[0])]
        own_out = attention(
            own_plan, own_lows, own_query, (0, rest_heads), own_pair, ((0, rest), (rest, 2 * rest)),
            own_next.reshape(chunk, ROWS, 2 * rest), own_after.reshape(chunk, ROWS, 2 * rest),
        )
        nears[0], own_out = lax.optimization_barrier((nears[0], own_out))
        for array in packed[1:]:
            nears.append(onward(lax.optimization_barrier((array, nears[-1]))[0]))
        done = []
        for i, (heads, bands) in enumerate(pieces):
            near, _ = lax.optimization_barrier((nears[i], done[:-1]))
            far = onward(pack(near, far_plan, far_slots, ((0, near.shape[2]),)))
            done.append(spread(attention(plan, plane_lows, query, heads, pair, bands, near, far)))
        return join_heads(done, own_out)

    shares = [[groups * chunk * share // 64 for share in room] for room in ROOMS]
    level = sum(
        ((near_sum > near) | (far_sum > far)).astype(jnp.int32) for near, far in shares[:-1]
    )
    return lax.switch(
        level, [functools.partial(run, room) for room in ROOMS],
        pair, query, near_plan, far_plan, plan, plane_lows, own_query, own_pair, own_next, own_after, own_plan, own_lows,
    )


def solution(mesh):
    return jax.shard_map(
        functools.partial(shards, mesh.shape["blk"], mesh.shape["uly"]),
        mesh=mesh,
        in_specs=(
            P(("blk", "uly"), None),
            P(("blk", "uly"), None),
            P(("blk", "uly"), None),
            P("blk"),
        ),
        out_specs=P(("blk", "uly"), None),
        check_vma=False,
    )
```

time: 292 us -> 184 us (0.63)
  waiting for transfers between devices: 116 us -> 69.6 us
  local copies, waits for them, and re-layouts: 58.2 us -> 12.7 us
  Pallas kernels: 0 us -> 43 us
  blocking collectives: 52.9 us -> 19.6 us
  matrix products: 22.5 us -> 0 us
  other arithmetic: 19.3 us -> 2.19 us
  starting transfers between devices: 21.2 us -> 28.7 us
  between operations: 0.09 us -> 6.57 us
    all_to_all x3 -> x4, waiting for transfers between devices: 116 us -> 10.7 us  [spread(): return lax.all_to_all(array, 'blk', split_axis=0, concat_axis=0, tiled=True)]
    ppermute x2 -> x6, waiting for transfers between devices: 0.01 us -> 58.9 us  [the longest x4 36.8 us: onward(): lax.ppermute(array, 'uly', [(i, (i + 1) % ring) for i in range(ring)])]
    pallas_call x0 -> x10, Pallas kernels: none -> 43 us  [the longest x3 24.7 us: attention(): pl.pallas_call(kernel, out_shape=jax.ShapeDtypeStruct((stretches, tokens,...]
    all_to_all x1, blocking collectives: 52.9 us -> 19.6 us  [spread(): return lax.all_to_all(array, 'blk', split_axis=0, concat_axis=0, tiled=True)]
    dot_general x4 -> x0, matrix products: 22.5 us -> none  [the longest x2 15.6 us: attend_span(): jnp.einsum('hqk,khd->qhd', weights, value_rows, preferred_element_type=jn...]
    unnamed x17 -> x2, local copies, waits for them, and re-layouts: 19.6 us -> 1.31 us
    all_to_all x5 -> x0, local copies, waits for them, and re-layouts: 17.8 us -> none  [the longest x2 6.66 us: shards(): lax.all_to_all(result, 'uly', split_axis=0, concat_axis=1, tiled=True)]
    dynamic_slice x8 -> x6, local copies, waits for them, and re-layouts: 11.6 us -> 1.95 us  [the longest x4 1.78 us: own(): return lax.dynamic_index_in_dim(per_chunk, me, 0, keepdims=False)]
  transfers between devices with their start and end apart: 5 -> 10, of which waited for: 3 -> 6; matrix products, arithmetic and copies ran while one was open for 9% -> 4% of each run, Pallas kernels for 0% -> 21%
where the time goes in v2:
time: 184 us; the launch traced here: 183 us
  waiting for transfers between devices  69.6 us (38%)
  Pallas kernels  43 us (23%)
  starting transfers between devices  28.7 us (16%)
  blocking collectives  19.6 us (11%)
  local copies, waits for them, and re-layouts  12.7 us (7%)
  between operations  6.57 us (4%)
  other arithmetic  2.19 us (1%)
    ppermute x4, waiting for transfers between devices, onward(): lax.ppermute(array, 'uly', [(i, (i + 1) % ring) for i in range(ring)])  36.8 us
    pallas_call x3, Pallas kernels, attention(): pl.pallas_call(kernel, out_shape=jax.ShapeDtypeStruct((stretches, tokens,...  24.7 us
    ppermute x2, waiting for transfers between devices, next_chunk(): lax.ppermute(array, ('blk', 'uly'), [(i, i + 1) for i in range(chunks - 1)])  22.1 us
    all_to_all x1, blocking collectives, spread(): return lax.all_to_all(array, 'blk', split_axis=0, concat_axis=0, tiled=True)  19.6 us
    all_to_all x4, starting transfers between devices, spread(): return lax.all_to_all(array, 'blk', split_axis=0, concat_axis=0, tiled=True)  18.8 us
    all_to_all x4, waiting for transfers between devices, spread(): return lax.all_to_all(array, 'blk', split_axis=0, concat_axis=0, tiled=True)  10.7 us
    ppermute x2, starting transfers between devices, next_chunk(): lax.ppermute(array, ('blk', 'uly'), [(i, i + 1) for i in range(chunks - 1)])  9.84 us
    pallas_call x2, Pallas kernels, split_heads(): pl.pallas_call(kernel, grid=(tokens // rows,), out_shape=[jax.ShapeDtypeS...  8.65 us
  transfers between devices with their start and end apart: 10, of which 6 were waited for; matrix products, arithmetic and copies ran while one was open for 4% of the time, Pallas kernels for 21%

profile of v2, /device:TPU:0, one launch (start us, length us, event | category | flops | bytes accessed | tf_op | source)
XLA Modules:
  0.0 183.1 jit_solution(3474524636503586713)
XLA Ops:
  0.0 1.3 broadcast_in_dim.73
  1.3 5.2 %all-to-all-start.15 = ((s32[8,1,1024]{2,1,0:T(1,128)}), s32[8,1,1024]{2,1,0:T(1,128)S(1)}, u32[]{:S(2)}, u32[]{:S(2)}) async-start(s32[8,1,1024]{2,1,0:T(1,128)} %broadcast_in_dim.73), calls=%async_computation.15 | async-start | bytes 65536 | tf_op jit(solution)/shard_map/all_to_all | solution.py:215
  6.5 4.8 %split_heads.2 = (bf16[8,256,768]{2,1,0:T(8,128)(2,1)}, bf16[1,256,2048]{2,1,0:T(8,128)(2,1)}) custom-call(bf16[256,4096]{1,0:T(8,128)(2,1)} %refs_0_.1, bf16[256,4096]{1,0:T(8,128)(2,1)} %refs_1_.1), custom_call_target="tpu_custom_call" | custom-call | bytes 8388608 | tf_op jit(solution)/shard_map/split_heads/pallas_call | solution.py:36
  11.3 4.5 %collective-permute-start.20 = (bf16[1,256,2048]{2,1,0:T(8,128)(2,1)}, bf16[1,256,2048]{2,1,0:T(8,128)(2,1)}, u32[]{:S(2)}, u32[]{:S(2)}) collective-permute-start(bf16[1,256,2048]{2,1,0:T(8,128)(2,1)} %get-tuple-element.219), channel_id=1, source_target_pairs={{0,1},{1,2},{2,3},{3,4},{4,5},{5,6},{6,7},{7,8},{8,9},{9,10},{10,1... | collective-permute-start | bytes 3145736 | tf_op jit(solution)/shard_map/ppermute | solution.py:221
  15.9 4.5 %all-to-all-start.16 = ((bf16[8,256,768]{2,1,0:T(8,128)(2,1)}), bf16[8,256,768]{2,1,0:T(8,128)(2,1)}, u32[]{:S(2)}, u32[]{:S(2)}) async-start(bf16[8,256,768]{2,1,0:T(8,128)(2,1)} %get-tuple-element.216), calls=%async_computation.16 | async-start | bytes 6291456 | tf_op jit(solution)/shard_map/all_to_all | solution.py:215
  20.8 0.1 fusion.1
  21.5 0.1 slice_reduce_fusion.4
  21.6 0.1 select_reduce_fusion.2
  21.7 0.1 slice_reduce_fusion.5
  21.9 0.1 slice_reduce_fusion.2
  22.0 0.1 slice_reduce_fusion.1
  22.1 16.0 %collective-permute-done.20 = bf16[1,256,2048]{2,1,0:T(8,128)(2,1)} collective-permute-done((bf16[1,256,2048]{2,1,0:T(8,128)(2,1)}, bf16[1,256,2048]{2,1,0:T(8,128)(2,1)}, u32[]{:S(2)}, u32[]{:S(2)}) %collective-permute-start.20) | collective-permute-done | bytes 1048608 | tf_op jit(solution)/shard_map/ppermute | solution.py:221
  38.1 5.4 %collective-permute-start.21 = (bf16[1,256,2048]{2,1,0:T(8,128)(2,1)}, bf16[1,256,2048]{2,1,0:T(8,128)(2,1)}, u32[]{:S(2)}, u32[]{:S(2)}) collective-permute-start(bf16[1,256,2048]{2,1,0:T(8,128)(2,1)} %collective-permute-done.20), channel_id=1, source_target_pairs={{0,1},{1,2},{2,3},{3,4},{4,5},{5,6},{6,7},{7,8},{8,9},{9,10},{10,1... | collective-permute-start | bytes 3145736 | tf_op jit(solution)/shard_map/ppermute | solution.py:221
  43.5 0.1 select_reduce_fusion
  43.6 0.6 dynamic_slice.34
  44.2 0.6 dynamic_slice.35
  44.8 0.6 dynamic_slice.36
  46.7 0.6 reduce_max.27
  49.9 0.6 reduce_max.28
  53.2 3.9 %split_heads.3 = (bf16[8,256,384]{2,1,0:T(8,128)(2,1)}, bf16[1,256,1024]{2,1,0:T(8,128)(2,1)}) custom-call(bf16[256,4096]{1,0:T(8,128)(2,1)} %refs_0_.2), custom_call_target="tpu_custom_call" | custom-call | bytes 4194304 | tf_op jit(solution)/shard_map/split_heads/pallas_call | solution.py:36
  57.1 1.9 %stack.31 = s32[5]{0:T(128)S(1)} concatenate(s32[1]{0:T(128)S(6)} %sub.133, s32[1]{0:T(128)} %dynamic_slice.34, s32[1]{0:T(128)S(6)} %sub.137, s32[1]{0:T(128)} %dynamic_slice.35, s32[1]{0:T(128)} %dynamic_slice.36), dimensions={0} | concatenate | bytes 40 | tf_op jit(solution)/shard_map/stack | solution.py:261
  59.0 0.1 select_reduce_fusion.3
  59.1 0.1 slice_reduce_fusion.3
  59.2 0.1 select_reduce_fusion.1
  59.4 6.1 %collective-permute-done.21 = bf16[1,256,2048]{2,1,0:T(8,128)(2,1)} collective-permute-done((bf16[1,256,2048]{2,1,0:T(8,128)(2,1)}, bf16[1,256,2048]{2,1,0:T(8,128)(2,1)}, u32[]{:S(2)}, u32[]{:S(2)}) %collective-permute-start.21) | collective-permute-done | bytes 1048608 | tf_op jit(solution)/shard_map/ppermute | solution.py:221
  65.6 10.7 %all-to-all-done.16 = bf16[8,256,768]{2,1,0:T(8,128)(2,1)} async-done(((bf16[8,256,768]{2,1,0:T(8,128)(2,1)}), bf16[8,256,768]{2,1,0:T(8,128)(2,1)}, u32[]{:S(2)}, u32[]{:S(2)}) %all-to-all-start.16) | async-done | bytes 3145760 | tf_op jit(solution)/shard_map/all_to_all | solution.py:215
  76.3 105.5 %conditional.1 = (bf16[256,4096]{1,0:T(8,128)(2,1)S(1)}) conditional(s32[]{:T(128)} %clamp.3, (bf16[8,256,768]{2,1,0:T(8,128)(2,1)}, s32[3,8]{1,0:T(4,128)S(1)}, bf16[8,256,384]{2,1,0:T(8,128)(2,1)}, bf16[1,256,2048]{2,1,0:T(8,128)(2,1)}, bf16[1,256,2048]{2,1,0:T(8,128)(2,1)}, /*index=5*/s32[5]{0:T(128)S(1)}, ...), branch_computations={%region_9.10_spmd, %region_10.11_spmd, %region_11.12_spmd, %region... | conditional | flops 1610612736 | bytes 122842688 | solution.py:302
  76.3 2.4 %pack_halo.24 = bf16[38,32,256]{2,1,0:T(8,128)(2,1)S(1)} custom-call(s32[3,8]{1,0:T(4,128)S(1)} %get-tuple-element.150.plan_ref, bf16[64,32,768]{2,1,0:T(8,128)(2,1)} %bitcast.51), custom_call_target="tpu_custom_call" | custom-call | bytes 1245184 | tf_op jit(solution)/shard_map/cond/branch_1_fun/pack_halo/pallas_call | solution.py:104
  78.7 0.4 copy-done.31
  79.1 1.9 %pack_halo.25 = bf16[38,32,512]{2,1,0:T(8,128)(2,1)} custom-call(s32[3,8]{1,0:T(4,128)S(1)} %get-tuple-element.150.plan_ref, bf16[64,32,768]{2,1,0:T(8,128)(2,1)S(1)} %bitcast.52), custom_call_target="tpu_custom_call" | custom-call | bytes 2490368 | tf_op jit(solution)/shard_map/cond/branch_1_fun/pack_halo/pallas_call | solution.py:104
  81.2 6.9 %attention.18.refs_2_ = bf16[1,256,1024]{2,1,0:T(8,128)(2,1)S(1)} custom-call(s32[5,1]{1,0:T(8,128)S(1)} %copy.33.plan_ref, f32[1,256,128]{2,1,0:T(8,128)S(1)} %broadcast_in_dim.94.lows_ref, bf16[1,256,1024]{2,1,0:T(8,128)(2,1)} %get-tuple-element.155.q_ref, bf16[1,256,2048]{2,1,0:T(8,128)(2,1)S(1)} %copy-done.35, bf16[8,32,2048]{2,1,0:T(8,128)(2,1)S(1)} %bitcast.60, ...), custom_call_target="tpu_custom_call" | custom-call | flops 402653184 | bytes 4194304 | tf_op jit(solution)/shard_map/cond/branch_1_fun/attention/pallas_call | solution.py:189
  88.2 0.8 copy-done.23
  89.0 7.4 %collective-permute-done.4.in_ref.near_ref = bf16[38,32,256]{2,1,0:T(8,128)(2,1)S(1)} collective-permute-done((bf16[38,32,256]{2,1,0:T(8,128)(2,1)S(1)}, bf16[38,32,256]{2,1,0:T(8,128)(2,1)S(1)}, u32[]{:S(2)}, u32[]{:S(2)}) %collective-permute-start.4) | collective-permute-done | bytes 622624 | tf_op jit(solution)/shard_map/cond/branch_1_fun/ppermute | solution.py:218
  96.4 5.7 %all-to-all-start.3 = ((bf16[8,256,384]{2,1,0:T(8,128)(2,1)}), bf16[8,256,384]{2,1,0:T(8,128)(2,1)S(1)}, u32[]{:S(2)}, u32[]{:S(2)}) async-start(bf16[8,256,384]{2,1,0:T(8,128)(2,1)} %get-tuple-element.152), calls=%async_computation.3 | async-start | bytes 3145728 | tf_op jit(solution)/shard_map/cond/branch_1_fun/all_to_all | solution.py:215
  102.1 1.5 pack_halo.26
  103.6 25.2 %collective-permute-done.6.in_ref.near_ref = bf16[38,32,512]{2,1,0:T(8,128)(2,1)S(1)} collective-permute-done((bf16[38,32,512]{2,1,0:T(8,128)(2,1)}, bf16[38,32,512]{2,1,0:T(8,128)(2,1)S(1)}, u32[]{:S(2)}, u32[]{:S(2)}) %collective-permute-start.6) | collective-permute-done | bytes 1245216 | tf_op jit(solution)/shard_map/cond/branch_1_fun/ppermute | solution.py:218
  128.8 1.5 pack_halo.27
  130.3 4.2 %collective-permute-done.5.far_ref = bf16[17,32,256]{2,1,0:T(8,128)(2,1)} collective-permute-done((bf16[17,32,256]{2,1,0:T(8,128)(2,1)}, bf16[17,32,256]{2,1,0:T(8,128)(2,1)}, u32[]{:S(2)}, u32[]{:S(2)}) %collective-permute-start.5) | collective-permute-done | bytes 278560 | tf_op jit(solution)/shard_map/cond/branch_1_fun/ppermute | solution.py:218
  134.5 0.3 broadcast_in_dim.99.lows_ref
  134.8 7.7 %attention.19 = bf16[8,256,128]{2,1,0:T(8,128)(2,1)S(1)} custom-call(s32[5,8]{1,0:T(8,128)S(1)} %get-tuple-element.147.plan_ref, f32[8,256,128]{2,1,0:T(8,128)S(1)} %broadcast_in_dim.99.lows_ref, bf16[8,256,384]{2,1,0:T(8,128)(2,1)S(1)} %all-to-all-done.3.q_ref, bf16[8,256,768]{2,1,0:T(8,128)(2,1)} %get-tuple-element.151.local_ref, ...), custom_call_target="tpu_custom_call" | custom-call | flops 402653184 | bytes 2998272 | tf_op jit(solution)/shard_map/cond/branch_1_fun/attention/pallas_call | solution.py:189
  142.5 0.8 copy-done.22
  143.3 3.5 %all-to-all-start.4 = ((bf16[8,256,128]{2,1,0:T(8,128)(2,1)}), bf16[8,256,128]{2,1,0:T(8,128)(2,1)S(1)}, u32[]{:S(2)}, u32[]{:S(2)}) async-start(bf16[8,256,128]{2,1,0:T(8,128)(2,1)} %copy-done.22), calls=%async_computation.4 | async-start | bytes 1048576 | tf_op jit(solution)/shard_map/cond/branch_1_fun/all_to_all | solution.py:215
  146.8 1.3 copy-done.7
  148.1 10.1 %attention.20 = bf16[8,256,256]{2,1,0:T(8,128)(2,1)S(1)} custom-call(s32[5,8]{1,0:T(8,128)S(1)} %get-tuple-element.147.plan_ref, f32[8,256,128]{2,1,0:T(8,128)S(1)} %broadcast_in_dim.99.lows_ref, bf16[8,256,384]{2,1,0:T(8,128)(2,1)S(1)} %all-to-all-done.3.q_ref, bf16[8,256,768]{2,1,0:T(8,128)(2,1)} %get-tuple-element.151.local_ref, ...), custom_call_target="tpu_custom_call" | custom-call | flops 805306368 | bytes 5996544 | tf_op jit(solution)/shard_map/cond/branch_1_fun/attention/pallas_call | solution.py:189
  158.2 1.0 copy-done.13
  159.2 19.6 %all_to_all.71.refs_1_ = bf16[8,256,256]{2,1,0:T(8,128)(2,1)} all-to-all(bf16[8,256,256]{2,1,0:T(8,128)(2,1)} %copy-done.13), channel_id=1, replica_groups=mesh['blk'=8,'uly'=4] {'blk'}, dimensions={0} | all-to-all | bytes 2097152 | tf_op jit(solution)/shard_map/cond/branch_1_fun/all_to_all | solution.py:215
  178.8 2.4 %join_heads.6 = bf16[256,4096]{1,0:T(8,128)(2,1)S(1)} custom-call(bf16[8,256,128]{2,1,0:T(8,128)(2,1)} %copy-done.43, bf16[8,256,256]{2,1,0:T(8,128)(2,1)} %all_to_all.71.refs_1_, bf16[1,256,1024]{2,1,0:T(8,128)(2,1)} %copy-done.23), custom_call_target="tpu_custom_call" | custom-call | bytes 4194304 | tf_op jit(solution)/shard_map/cond/branch_1_fun/join_heads/pallas_call | solution.py:70
  181.8 1.3 copy-done.41
  (53 shorter events, 1.7 us)
Async XLA Ops:
  1.3 14.6 %all-to-all-start.15 = ((s32[8,1,1024]{2,1,0:T(1,128)}), s32[8,1,1024]{2,1,0:T(1,128)S(1)}, u32[]{:S(2)}, u32[]{:S(2)}) async-start(s32[8,1,1024]{2,1,0:T(1,128)} %broadcast_in_dim.73), calls=%async_computation.15 | async-start | bytes 65536 | tf_op jit(solution)/shard_map/all_to_all | solution.py:215
  11.3 26.9 %collective-permute-start.20 = (bf16[1,256,2048]{2,1,0:T(8,128)(2,1)}, bf16[1,256,2048]{2,1,0:T(8,128)(2,1)}, u32[]{:S(2)}, u32[]{:S(2)}) collective-permute-start(bf16[1,256,2048]{2,1,0:T(8,128)(2,1)} %get-tuple-element.219), channel_id=1, source_target_pairs={{0,1},{1,2},{2,3},{3,4},{4,5},{5,6},{6,7},{7,8},{8,9},{9,10},{10,1... | collective-permute-start | bytes 3145736 | tf_op jit(solution)/shard_map/ppermute | solution.py:221
  15.9 60.3 %all-to-all-start.16 = ((bf16[8,256,768]{2,1,0:T(8,128)(2,1)}), bf16[8,256,768]{2,1,0:T(8,128)(2,1)}, u32[]{:S(2)}, u32[]{:S(2)}) async-start(bf16[8,256,768]{2,1,0:T(8,128)(2,1)} %get-tuple-element.216), calls=%async_computation.16 | async-start | bytes 6291456 | tf_op jit(solution)/shard_map/all_to_all | solution.py:215
  38.1 27.4 %collective-permute-start.21 = (bf16[1,256,2048]{2,1,0:T(8,128)(2,1)}, bf16[1,256,2048]{2,1,0:T(8,128)(2,1)}, u32[]{:S(2)}, u32[]{:S(2)}) collective-permute-start(bf16[1,256,2048]{2,1,0:T(8,128)(2,1)} %collective-permute-done.20), channel_id=1, source_target_pairs={{0,1},{1,2},{2,3},{3,4},{4,5},{5,6},{6,7},{7,8},{8,9},{9,10},{10,1... | collective-permute-start | bytes 3145736 | tf_op jit(solution)/shard_map/ppermute | solution.py:221
  76.3 2.8 %copy-start.31 = (bf16[8,256,768]{2,1,0:T(8,128)(2,1)S(1)}, bf16[8,256,768]{2,1,0:T(8,128)(2,1)}, u32[]{:S(2)}) copy-start(bf16[8,256,768]{2,1,0:T(8,128)(2,1)} %get-tuple-element.151.local_ref) | copy-start | bytes 9437188 | tf_op jit(solution)/shard_map/cond
  78.6 2.6 %copy-start.35 = (bf16[1,256,2048]{2,1,0:T(8,128)(2,1)S(1)}, bf16[1,256,2048]{2,1,0:T(8,128)(2,1)}, u32[]{:S(2)}) copy-start(bf16[1,256,2048]{2,1,0:T(8,128)(2,1)} %get-tuple-element.156.local_ref) | copy-start | bytes 3145732 | tf_op jit(solution)/shard_map/cond
  78.6 2.6 %copy-start.38 = (bf16[1,256,2048]{2,1,0:T(8,128)(2,1)S(1)}, bf16[1,256,2048]{2,1,0:T(8,128)(2,1)}, u32[]{:S(2)}) copy-start(bf16[1,256,2048]{2,1,0:T(8,128)(2,1)} %get-tuple-element.157) | copy-start | bytes 3145732 | tf_op jit(solution)/shard_map/cond
  78.7 17.8 %collective-permute-start.4 = (bf16[38,32,256]{2,1,0:T(8,128)(2,1)S(1)}, bf16[38,32,256]{2,1,0:T(8,128)(2,1)S(1)}, u32[]{:S(2)}, u32[]{:S(2)}) collective-permute-start(bf16[38,32,256]{2,1,0:T(8,128)(2,1)S(1)} %pack_halo.24), channel_id=1, source_target_pairs={{0,1},{1,2},{2,3},{3,0},{4,5},{5,6},{6,7},{7,4},{8,9},{9,10},{10,1... | collective-permute-start | bytes 1867784 | tf_op jit(solution)/shard_map/cond/branch_1_fun/ppermute | solution.py:218
  88.1 0.9 copy-start.23
  96.4 32.3 %collective-permute-start.6 = (bf16[38,32,512]{2,1,0:T(8,128)(2,1)}, bf16[38,32,512]{2,1,0:T(8,128)(2,1)S(1)}, u32[]{:S(2)}, u32[]{:S(2)}) collective-permute-start(bf16[38,32,512]{2,1,0:T(8,128)(2,1)} %pack_halo.25), channel_id=1, source_target_pairs={{0,1},{1,2},{2,3},{3,0},{4,5},{5,6},{6,7},{7,4},{8,9},{9,10},{10,1... | collective-permute-start | bytes 3735560 | tf_op jit(solution)/shard_map/cond/branch_1_fun/ppermute | solution.py:218
  96.4 38.0 %all-to-all-start.3 = ((bf16[8,256,384]{2,1,0:T(8,128)(2,1)}), bf16[8,256,384]{2,1,0:T(8,128)(2,1)S(1)}, u32[]{:S(2)}, u32[]{:S(2)}) async-start(bf16[8,256,384]{2,1,0:T(8,128)(2,1)} %get-tuple-element.152), calls=%async_computation.3 | async-start | bytes 3145728 | tf_op jit(solution)/shard_map/cond/branch_1_fun/all_to_all | solution.py:215
  103.5 30.9 %collective-permute-start.5 = (bf16[17,32,256]{2,1,0:T(8,128)(2,1)}, bf16[17,32,256]{2,1,0:T(8,128)(2,1)}, u32[]{:S(2)}, u32[]{:S(2)}) collective-permute-start(bf16[17,32,256]{2,1,0:T(8,128)(2,1)} %pack_halo.26), channel_id=1, source_target_pairs={{0,1},{1,2},{2,3},{3,0},{4,5},{5,6},{6,7},{7,4},{8,9},{9,10},{10,1... | collective-permute-start | bytes 835592 | tf_op jit(solution)/shard_map/cond/branch_1_fun/ppermute | solution.py:218
  128.8 5.7 %copy-start.6 = (bf16[38,32,512]{2,1,0:T(8,128)(2,1)}, bf16[38,32,512]{2,1,0:T(8,128)(2,1)S(1)}, u32[]{:S(2)}) copy-start(bf16[38,32,512]{2,1,0:T(8,128)(2,1)S(1)} %collective-permute-done.6.in_ref.near_ref) | copy-start | bytes 3735556 | tf_op jit(solution)/shard_map/cond
  130.3 16.5 %collective-permute-start.7 = (bf16[17,32,512]{2,1,0:T(8,128)(2,1)}, bf16[17,32,512]{2,1,0:T(8,128)(2,1)}, u32[]{:S(2)}, u32[]{:S(2)}) collective-permute-start(bf16[17,32,512]{2,1,0:T(8,128)(2,1)} %pack_halo.27), channel_id=1, source_target_pairs={{0,1},{1,2},{2,3},{3,0},{4,5},{5,6},{6,7},{7,4},{8,9},{9,10},{10,1... | collective-permute-start | bytes 1671176 | tf_op jit(solution)/shard_map/cond/branch_1_fun/ppermute | solution.py:218
  142.5 0.8 copy-start.22
  143.3 15.9 %all-to-all-start.4 = ((bf16[8,256,128]{2,1,0:T(8,128)(2,1)}), bf16[8,256,128]{2,1,0:T(8,128)(2,1)S(1)}, u32[]{:S(2)}, u32[]{:S(2)}) async-start(bf16[8,256,128]{2,1,0:T(8,128)(2,1)} %copy-done.22), calls=%async_computation.4 | async-start | bytes 1048576 | tf_op jit(solution)/shard_map/cond/branch_1_fun/all_to_all | solution.py:215
  146.8 1.3 copy-start.7
  158.2 1.0 copy-start.13
  159.2 19.6 %copy-start.43 = (bf16[8,256,128]{2,1,0:T(8,128)(2,1)}, bf16[8,256,128]{2,1,0:T(8,128)(2,1)S(1)}, u32[]{:S(2)}) copy-start(bf16[8,256,128]{2,1,0:T(8,128)(2,1)S(1)} %all-to-all-done.4.refs_0_) | copy-start | bytes 1572868 | tf_op jit(solution)/shard_map/cond
  181.8 1.3 copy-start.41
